TPU v7x, 32 devices: a whole 2x2x4 slice. The times are simulated.
32 devices in a mesh: row: 8 (over z, core), col: 4 (over y, x).
Axes of the slice: x: 2, y: 2, z: 4, core: 2. Of those that a mesh axis runs over, the one named last changes fastest.
Arguments:
- tokens: bfloat16 [256, 8192], P('col', 'row'), may hold values from -6 to 6
- gate_weight: bfloat16 [8192, 26624], P('row', 'col'), may hold values from -0.0625 to 0.0625
- up_weight: bfloat16 [8192, 26624], P('row', 'col'), may hold values from -0.0625 to 0.0625
- down_weight: bfloat16 [26624, 8192], P('col', 'row'), may hold values from -0.0390625 to 0.0390625
- cotangent: bfloat16 [256, 8192], P('col', 'row'), may hold values from -3 to 3
Outputs:
- mixed: bfloat16 [256, 8192], P('col', 'row')
- grad_tokens: bfloat16 [256, 8192], P('col', 'row')
- grad_gate: bfloat16 [8192, 26624], P('row', 'col')
- grad_up: bfloat16 [8192, 26624], P('row', 'col')
- grad_down: bfloat16 [26624, 8192], P('col', 'row')
All inputs are finite; a program needn't handle non-finite values.
Results may differ from a plain program's by a relative error of at most 0.019.
Values may be sent and summed in bfloat16 or wider, within the bound.
No kernel may reach another device: no remote copies, remote signals or barrier semaphores. Data moves between devices by JAX's collectives and lax.ppermute only.
A program may use at most 192 MiB of HBM per device.

v0:
```python
import functools

import jax
import jax.numpy as jnp
from jax import lax
from jax.experimental import pallas as pl
from jax.experimental.pallas import tpu as pltpu
from jax.sharding import PartitionSpec as P

F32 = jnp.float32
BF16 = jnp.bfloat16
MOST_CHUNKS = 9
PRODUCT_VMEM = 40 * 1024 * 1024
SMALL_VMEM = 10 * 1024 * 1024
ANYWHERE = pl.BlockSpec(memory_space=pl.ANY)


def unit_of(hidden_units):
    return 256 if hidden_units % 256 == 0 else 128


def chunks_of(hidden_units):
    unit = unit_of(hidden_units)
    width = -(-(hidden_units // unit) // MOST_CHUNKS) * unit
    return [(s, min(width, hidden_units - s)) for s in range(0, hidden_units, width)]


def tile_of(width):
    return 256 if width % 256 == 0 else 128


def whole(shape):
    return pl.BlockSpec(shape, lambda i: (0,) * len(shape))


class Order:
    def __init__(self):
        self.last = None

    def call(self, kernel, grid, in_specs, out_specs, out_shape, aliases, vmem, cost, name, *args):
        extra = [] if self.last is None else [self.last]

        def body(*refs):
            kernel(*refs[: len(args)], *refs[len(args) + len(extra) :])

        out = pl.pallas_call(
            body,
            grid=grid,
            in_specs=list(in_specs) + [ANYWHERE] * len(extra),
            out_specs=out_specs,
            out_shape=out_shape,
            input_output_aliases=aliases,
            compiler_params=pltpu.CompilerParams(vmem_limit_bytes=vmem),
            cost_estimate=pl.CostEstimate(flops=cost, bytes_accessed=cost, transcendentals=0),
            name=name,
        )(*args, *extra)
        self.last = out[0]
        return out


def forward_kernel(x_ref, ct_ref, gate_ref, up_ref, down_ref, mine_ref, theirs_ref):
    half = mine_ref.shape[1]
    sums = (
        jnp.dot(x_ref[...], gate_ref[...], preferred_element_type=F32),
        jnp.dot(x_ref[...], up_ref[...], preferred_element_type=F32),
        jnp.dot(down_ref[...], ct_ref[...], preferred_element_type=F32).T,
    )
    for index, value in enumerate(sums):
        mine_ref[index] = value[:half].astype(BF16)
        theirs_ref[index] = value[half:].astype(BF16)


def forward(order, x, ct, gate, up, down, start, width):
    tokens, depth = x.shape
    tile = tile_of(width)
    first = start // tile
    half = tokens // 2
    part = jax.ShapeDtypeStruct((3, half, width), BF16)
    column = pl.BlockSpec((depth, tile), lambda i: (0, first + i))
    row = pl.BlockSpec((tile, depth), lambda i: (first + i, 0))
    piece = pl.BlockSpec((3, half, tile), lambda i: (0, 0, i))
    return order.call(
        forward_kernel,
        (width // tile,),
        [whole(x.shape), whole(ct.shape), column, column, row],
        [piece, piece],
        [part, part],
        {},
        PRODUCT_VMEM,
        1000,
        "forward_sums",
        x, ct, gate, up, down,
    )


def elementwise(order, kernel, name, *args):
    _, half, width = args[0].shape
    tile = tile_of(width)
    piece = pl.BlockSpec((3, half, tile), lambda i: (0, 0, i))
    specs = [piece if a.ndim == 3 else pl.BlockSpec(memory_space=pltpu.SMEM) for a in args]
    shape = jax.ShapeDtypeStruct(args[0].shape, BF16)
    return order.call(
        kernel, (width // tile,), specs, [piece], [shape], {}, SMALL_VMEM, 1000, name, *args
    )[0]


def add_kernel(left_ref, right_ref, out_ref):
    out_ref[...] = (left_ref[...].astype(F32) + right_ref[...].astype(F32)).astype(BF16)


def choose_kernel(left_ref, flag_ref, right_ref, out_ref):
    @pl.when(flag_ref[0] == 0)
    def _():
        out_ref[...] = left_ref[...]

    @pl.when(flag_ref[0] != 0)
    def _():
        out_ref[...] = right_ref[...]


def activation_kernel(left_ref, right_ref, out_ref):
    gate_sum, up_sum, back_sum = (
        left_ref[i].astype(F32) + right_ref[i].astype(F32) for i in range(3)
    )
    sigma = jax.nn.sigmoid(gate_sum)
    silu = gate_sum * sigma
    out_ref[0] = (silu * up_sum).astype(BF16)
    out_ref[1] = (back_sum * up_sum * sigma * (1.0 + gate_sum * (1.0 - sigma))).astype(BF16)
    out_ref[2] = (back_sum * silu).astype(BF16)


def joined(mine_ref, other_ref):
    return [jnp.concatenate([mine_ref[i], other_ref[i]], axis=0) for i in range(3)]


def token_products(acts, weight_refs, before_refs, mixed_ref, inputs_ref):
    gate_ref, up_ref, down_ref = weight_refs

    @pl.when(pl.program_id(0) == 0)
    def _():
        if not before_refs:
            mixed_ref[...] = jnp.zeros_like(mixed_ref)
            inputs_ref[...] = jnp.zeros_like(inputs_ref)

    hidden, gate_act, up_act = acts
    mixed_ref[...] += jnp.dot(hidden, down_ref[...], preferred_element_type=F32)
    inputs_ref[...] += jnp.dot(
        gate_ref[...], gate_act.T, preferred_element_type=F32
    ) + jnp.dot(up_ref[...], up_act.T, preferred_element_type=F32)


def weight_products(acts, xt_ref, c_ref, grad_gate_ref, grad_up_ref, grad_down_ref):
    hidden, gate_act, up_act = acts
    grad_gate_ref[...] = jnp.dot(xt_ref[...], gate_act, preferred_element_type=F32).astype(BF16)
    grad_up_ref[...] = jnp.dot(xt_ref[...], up_act, preferred_element_type=F32).astype(BF16)
    grad_down_ref[...] = jnp.dot(hidden.T, c_ref[...], preferred_element_type=F32).astype(BF16)


def backward(order, mine, other, xt, c, weights, start, totals, grads, parts):
    _, half, width = mine.shape
    tile = tile_of(width)
    first = start // tile
    piece = pl.BlockSpec((3, half, tile), lambda i: (0, 0, i))
    column = pl.BlockSpec((c.shape[1], tile), lambda i: (0, first + i))
    row = pl.BlockSpec((tile, c.shape[1]), lambda i: (first + i, 0))
    resident = pl.BlockSpec(memory_space=pltpu.VMEM)
    with_tokens, with_weights = "tokens" in parts, "weights" in parts
    specs, args, out_specs, shapes, aliases = [piece, piece], [mine, other], [], [], {}
    if with_tokens:
        specs += [column, column, row]
        args += weights
        for index, total in enumerate(totals or ()):
            aliases[len(args)] = index
            specs += [resident]
            args += [total]
        out_specs += [resident, resident]
        shapes += [jax.ShapeDtypeStruct(a.shape, F32) for a in (c, xt)]
    n_token_args = len(args)
    if with_weights:
        specs += [whole(xt.shape), whole(c.shape)]
        args += [xt, c]
        for index, grad in enumerate(grads or ()):
            aliases[len(args)] = len(out_specs) + index
            specs += [ANYWHERE]
            args += [grad]
        out_specs += [column, column, row]
        shapes += [jax.ShapeDtypeStruct(w.shape, BF16) for w in weights]

    def kernel(*refs):
        ins, outs = refs[: len(args)], refs[len(args) :]
        acts = joined(*ins[:2])
        if with_tokens:
            token_products(acts, ins[2:5], ins[5:n_token_args], *outs[:2])
        if with_weights:
            weight_products(acts, *ins[n_token_args : n_token_args + 2], *outs[-3:])

    out = order.call(
        kernel, (width // tile,), specs, out_specs, shapes, aliases, PRODUCT_VMEM, 1000,
        "backward_products", *args,
    )
    return (out[:2] if with_tokens else totals), (out[-3:] if with_weights else grads)


def both_cores(pairs):
    return [(2 * a + core, 2 * b + core) for a, b in pairs for core in range(2)]


def shards(n_row, n_col, tokens, gate_weight, up_weight, down_weight, cotangent):
    chips = n_row // 2
    middle = chips // 2
    core = lax.axis_index("row") % 2
    chip = lax.axis_index("row") // 2
    siblings = [(r, r ^ 1) for r in range(n_row)]
    inward = [both_cores([(j, j + 1), (chips - 1 - j, chips - 2 - j)]) for j in range(middle - 1)]
    across = both_cores([(middle - 1, middle), (middle, middle - 1)])
    flags = [
        jnp.where((chip == j) | (chip == chips - 1 - j), 1, 0).astype(jnp.int32).reshape(1)
        for j in range(middle - 1)
    ]
    weights = [gate_weight, up_weight, down_weight]

    def gather(block):
        blocks = [block] + [
            lax.ppermute(block, "col", [(s, s ^ j) for s in range(n_col)]) for j in range(1, n_col)
        ]
        low = jnp.concatenate(blocks[: n_col // 2], axis=0)
        high = jnp.concatenate(blocks[n_col // 2 :], axis=0)
        return jnp.concatenate(
            [jnp.where(core == 0, low, high), jnp.where(core == 0, high, low)], axis=0
        )

    x = gather(tokens)
    c = gather(cotangent)
    xt, ct = x.T, c.T

    order = Order()
    chunks = chunks_of(gate_weight.shape[1])
    count = len(chunks)
    swapped, partial, arrived, acts, other = {}, {}, {}, {}, {}
    state = [None, None]

    def step_sums(k):
        if 0 <= k < count:
            mine, theirs = forward(order, x, ct, *weights, *chunks[k])
            swapped[k] = (mine, lax.ppermute(theirs, "row", siblings))

    def step_chip(k):
        if 0 <= k < count:
            partial[k] = elementwise(order, add_kernel, "chip_sum", *swapped.pop(k))
            if inward:
                arrived[k] = lax.ppermute(partial[k], "row", inward[0])

    def step_half(k):
        if 0 <= k < count:
            for hop in range(len(inward)):
                partial[k] = elementwise(order, add_kernel, "half_sum", partial[k], arrived[k])
                if hop + 1 < len(inward):
                    arrived[k] = lax.ppermute(partial[k], "row", inward[hop + 1])
            arrived[k] = lax.ppermute(partial[k], "row", across)

    def step_act(k):
        if 0 <= k < count:
            acts[k] = elementwise(
                order, activation_kernel, "activations", partial.pop(k), arrived.pop(k)
            )
            if inward:
                back = [(t, s) for s, t in inward[-1]]
                arrived[k] = lax.ppermute(acts[k], "row", back)

    def step_choose(k):
        if 0 <= k < count:
            for hop in reversed(range(len(inward))):
                acts[k] = elementwise(
                    order, choose_kernel, "choose", acts[k], flags[hop], arrived[k]
                )
                if hop > 0:
                    back = [(t, s) for s, t in inward[hop - 1]]
                    arrived[k] = lax.ppermute(acts[k], "row", back)
            other[k] = lax.ppermute(acts[k], "row", siblings)

    def step_back(k, parts=("tokens", "weights")):
        if 0 <= k < count:
            state[0], state[1] = backward(
                order, acts[k], other[k], xt, c, weights, chunks[k][0], *state, parts
            )

    step_sums(0)
    step_sums(1)
    step_chip(0)
    step_sums(2)
    step_chip(1)
    step_sums(3)
    for k in range(count + 2):
        step_half(k)
        step_act(k - 1)
        step_chip(k + 2)
        step_sums(k + 4)
        if k - 3 < count - 1:
            step_back(k - 3)
        step_choose(k - 2)
    step_back(count - 1, ("tokens",))
    mixed, inputs = state[0]
    total = jnp.stack([mixed, inputs.T])

    half = total.shape[1] // 2
    block = total.shape[1] // n_col
    total = total.astype(BF16)
    ordered = jnp.where(
        core == 0, total, jnp.concatenate([total[:, half:], total[:, :half]], axis=1)
    )
    out = ordered[:, :block].astype(F32)
    for j in range(1, n_col):
        piece = ordered[:, j * block : (j + 1) * block]
        out += lax.ppermute(piece, "col", [(s, s ^ j) for s in range(n_col)]).astype(F32)
    out = out.astype(BF16)
    step_back(count - 1, ("weights",))
    return out[0], out[1], *state[1]


def solution(mesh):
    in_specs = (P("col", "row"), P("row", "col"), P("row", "col"), P("col", "row"), P("col", "row"))
    out_specs = (
        P("col", "row"),
        P("col", "row"),
        P("row", "col"),
        P("row", "col"),
        P("col", "row"),
    )
    return jax.shard_map(
        functools.partial(shards, mesh.shape["row"], mesh.shape["col"]),
        mesh=mesh,
        in_specs=in_specs,
        out_specs=out_specs,
        check_vma=False,
    )
```

profile of v0, /device:TPU:0, one launch (start us, length us, event | category | flops | bytes accessed | tf_op | source)
XLA Modules:
  0.0 298.5 jit_solution(16085985591914984144)
XLA Ops:
  20.4 4.3 %forward_sums.9 = (bf16[3,128,768]{2,1,0:T(8,128)(2,1)S(1)}, bf16[3,128,768]{2,1,0:T(8,128)(2,1)S(1)}) custom-call(bf16[256,1024]{1,0:T(8,128)(2,1)S(1)} %get-tuple-element.146.refs_0_, bf16[1024,256]{1,0:T(8,128)(2,1)S(1)} %copy.59.refs_1_, bf16[1024,6656]{1,0:T(8,128)(2,1)} %refs_2_.35, bf16[1024,6656]{1,0:T(8,128)(2,1)} %refs_3_.35, ...), custom_call_target="tpu_custom_call" | custom-call | flops 1000 | bytes 1000 | tf_op jit(solution)/shard_map/forward_sums/pallas_call | solution.py:46
  39.4 4.9 %forward_sums.12 = (bf16[3,128,768]{2,1,0:T(8,128)(2,1)S(1)}, bf16[3,128,768]{2,1,0:T(8,128)(2,1)}) custom-call(bf16[256,1024]{1,0:T(8,128)(2,1)S(1)} %get-tuple-element.146.refs_0_, bf16[1024,256]{1,0:T(8,128)(2,1)S(1)} %copy.59.refs_1_, bf16[1024,6656]{1,0:T(8,128)(2,1)} %refs_2_.35, bf16[1024,6656]{1,0:T(8,128)(2,1)} %refs_3_.35, ...), custom_call_target="tpu_custom_call" | custom-call | flops 1000 | bytes 1000 | tf_op jit(solution)/shard_map/forward_sums/pallas_call | solution.py:46
  49.8 4.8 %forward_sums.13 = (bf16[3,128,768]{2,1,0:T(8,128)(2,1)S(1)}, bf16[3,128,768]{2,1,0:T(8,128)(2,1)}) custom-call(bf16[256,1024]{1,0:T(8,128)(2,1)S(1)} %get-tuple-element.146.refs_0_, bf16[1024,256]{1,0:T(8,128)(2,1)S(1)} %copy.59.refs_1_, bf16[1024,6656]{1,0:T(8,128)(2,1)} %refs_2_.35, bf16[1024,6656]{1,0:T(8,128)(2,1)} %refs_3_.35, ...), custom_call_target="tpu_custom_call" | custom-call | flops 1000 | bytes 1000 | tf_op jit(solution)/shard_map/forward_sums/pallas_call | solution.py:46
  54.6 8.0 %collective-permute-start.13 = (bf16[3,128,768]{2,1,0:T(8,128)(2,1)}, bf16[3,128,768]{2,1,0:T(8,128)(2,1)}, u32[]{:S(2)}, u32[]{:S(2)}) collective-permute-start(bf16[3,128,768]{2,1,0:T(8,128)(2,1)} %chip_sum.11.refs_5_.refs_0_), channel_id=1, source_target_pairs={{0,8},{4,12},{24,16},{28,20},{1,9},{5,13},{25,17},{29,21},{2,10},{... | collective-permute-start | bytes 1769480 | tf_op jit(solution)/shard_map/ppermute | solution.py:251
  70.3 4.9 %forward_sums.14 = (bf16[3,128,768]{2,1,0:T(8,128)(2,1)S(1)}, bf16[3,128,768]{2,1,0:T(8,128)(2,1)}) custom-call(bf16[256,1024]{1,0:T(8,128)(2,1)S(1)} %get-tuple-element.146.refs_0_, bf16[1024,256]{1,0:T(8,128)(2,1)S(1)} %copy.59.refs_1_, bf16[1024,6656]{1,0:T(8,128)(2,1)} %refs_2_.35, bf16[1024,6656]{1,0:T(8,128)(2,1)} %refs_3_.35, ...), custom_call_target="tpu_custom_call" | custom-call | flops 1000 | bytes 1000 | tf_op jit(solution)/shard_map/forward_sums/pallas_call | solution.py:46
  75.2 6.1 %collective-permute-start.17 = (bf16[3,128,768]{2,1,0:T(8,128)(2,1)}, bf16[3,128,768]{2,1,0:T(8,128)(2,1)}, u32[]{:S(2)}, u32[]{:S(2)}) collective-permute-start(bf16[3,128,768]{2,1,0:T(8,128)(2,1)} %chip_sum.12.refs_5_.refs_0_), channel_id=1, source_target_pairs={{0,8},{4,12},{24,16},{28,20},{1,9},{5,13},{25,17},{29,21},{2,10},{... | collective-permute-start | bytes 1769480 | tf_op jit(solution)/shard_map/ppermute | solution.py:251
  102.6 5.4 %collective-permute-start.20 = (bf16[3,128,768]{2,1,0:T(8,128)(2,1)}, bf16[3,128,768]{2,1,0:T(8,128)(2,1)S(1)}, u32[]{:S(2)}, u32[]{:S(2)}) collective-permute-start(bf16[3,128,768]{2,1,0:T(8,128)(2,1)} %chip_sum.13.refs_5_.refs_0_), channel_id=1, source_target_pairs={{0,8},{4,12},{24,16},{28,20},{1,9},{5,13},{25,17},{29,21},{2,10},{... | collective-permute-start | bytes 1769480 | tf_op jit(solution)/shard_map/ppermute | solution.py:251
  121.5 6.9 %backward_products.10 = (f32[256,1024]{1,0:T(8,128)S(1)}, f32[1024,256]{1,0:T(8,128)S(1)}, bf16[1024,6656]{1,0:T(8,128)(2,1)}, bf16[1024,6656]{1,0:T(8,128)(2,1)}, bf16[6656,1024]{1,0:T(8,128)(2,1)}) custom-call(bf16[3,128,768]{2,1,0:T(8,128)(2,1)} %choose.9.refs_2_.refs_0_, bf16[3,128,768]{2,1,0:T(8,128)(2,1)S(1)} %copy-done.15, ...), custom_call_target="tpu_custom_call" | custom-call | flops 1000 | bytes 1000 | tf_op jit(solution)/shard_map/backward_products/pallas_call | solution.py:46
  132.4 4.6 %collective-permute-start.26 = (bf16[3,128,768]{2,1,0:T(8,128)(2,1)S(1)}, bf16[3,128,768]{2,1,0:T(8,128)(2,1)S(1)}, u32[]{:S(2)}, u32[]{:S(2)}) collective-permute-start(bf16[3,128,768]{2,1,0:T(8,128)(2,1)S(1)} %chip_sum.14.refs_5_.refs_0_), channel_id=1, source_target_pairs={{0,8},{4,12},{24,16},{28,20},{1,9},{5,13},{25,17},{29,21},{2,10},{... | collective-permute-start | bytes 1769480 | tf_op jit(solution)/shard_map/ppermute | solution.py:251
  143.8 6.0 %backward_products.11 = (f32[256,1024]{1,0:T(8,128)S(1)}, f32[1024,256]{1,0:T(8,128)S(1)}, bf16[1024,6656]{1,0:T(8,128)(2,1)}, bf16[1024,6656]{1,0:T(8,128)(2,1)}, bf16[6656,1024]{1,0:T(8,128)(2,1)}) custom-call(bf16[3,128,768]{2,1,0:T(8,128)(2,1)S(1)} %choose.10.refs_2_.refs_0_, ...), custom_call_target="tpu_custom_call", output_to_operand_aliasing={{0}: (5, {}), {1}: (6, {}), {2}: (9, {}), {3}: (10, {}), {4... | custom-call | flops 1000 | bytes 1000 | tf_op jit(solution)/shard_map/backward_products/pallas_call | solution.py:46
  151.9 4.6 %collective-permute-start.30 = (bf16[3,128,768]{2,1,0:T(8,128)(2,1)S(1)}, bf16[3,128,768]{2,1,0:T(8,128)(2,1)S(1)}, u32[]{:S(2)}, u32[]{:S(2)}) collective-permute-start(bf16[3,128,768]{2,1,0:T(8,128)(2,1)S(1)} %chip_sum.15.refs_5_.refs_0_), channel_id=1, source_target_pairs={{0,8},{4,12},{24,16},{28,20},{1,9},{5,13},{25,17},{29,21},{2,10},{... | collective-permute-start | bytes 1769480 | tf_op jit(solution)/shard_map/ppermute | solution.py:251
  158.5 6.0 %backward_products.12 = (f32[256,1024]{1,0:T(8,128)S(1)}, f32[1024,256]{1,0:T(8,128)S(1)}, bf16[1024,6656]{1,0:T(8,128)(2,1)}, bf16[1024,6656]{1,0:T(8,128)(2,1)}, bf16[6656,1024]{1,0:T(8,128)(2,1)}) custom-call(bf16[3,128,768]{2,1,0:T(8,128)(2,1)S(1)} %choose.11.refs_2_.refs_0_, ...), custom_call_target="tpu_custom_call", output_to_operand_aliasing={{0}: (5, {}), {1}: (6, {}), {2}: (9, {}), {3}: (10, {}), {4... | custom-call | flops 1000 | bytes 1000 | tf_op jit(solution)/shard_map/backward_products/pallas_call | solution.py:46
  176.2 6.0 %backward_products.13 = (f32[256,1024]{1,0:T(8,128)S(1)}, f32[1024,256]{1,0:T(8,128)S(1)}, bf16[1024,6656]{1,0:T(8,128)(2,1)}, bf16[1024,6656]{1,0:T(8,128)(2,1)}, bf16[6656,1024]{1,0:T(8,128)(2,1)}) custom-call(bf16[3,128,768]{2,1,0:T(8,128)(2,1)S(1)} %choose.12.refs_2_.refs_0_, ...), custom_call_target="tpu_custom_call", output_to_operand_aliasing={{0}: (5, {}), {1}: (6, {}), {2}: (9, {}), {3}: (10, {}), {4... | custom-call | flops 1000 | bytes 1000 | tf_op jit(solution)/shard_map/backward_products/pallas_call | solution.py:46
  189.0 6.0 %backward_products.14 = (f32[256,1024]{1,0:T(8,128)S(1)}, f32[1024,256]{1,0:T(8,128)S(1)}, bf16[1024,6656]{1,0:T(8,128)(2,1)}, bf16[1024,6656]{1,0:T(8,128)(2,1)}, bf16[6656,1024]{1,0:T(8,128)(2,1)}) custom-call(bf16[3,128,768]{2,1,0:T(8,128)(2,1)S(1)} %choose.13.refs_2_.refs_0_, ...), custom_call_target="tpu_custom_call", output_to_operand_aliasing={{0}: (5, {}), {1}: (6, {}), {2}: (9, {}), {3}: (10, {}), {4... | custom-call | flops 1000 | bytes 1000 | tf_op jit(solution)/shard_map/backward_products/pallas_call | solution.py:46
  195.0 8.7 %collective-permute-done.36.refs_2_ = bf16[3,128,768]{2,1,0:T(8,128)(2,1)S(1)} collective-permute-done((bf16[3,128,768]{2,1,0:T(8,128)(2,1)S(1)}, bf16[3,128,768]{2,1,0:T(8,128)(2,1)S(1)}, u32[]{:S(2)}, u32[]{:S(2)}) %collective-permute-start.36) | collective-permute-done | bytes 589856 | tf_op jit(solution)/shard_map/ppermute | solution.py:268
  205.4 4.6 %collective-permute-start.35 = (bf16[3,128,512]{2,1,0:T(8,128)(2,1)S(1)}, bf16[3,128,512]{2,1,0:T(8,128)(2,1)S(1)}, u32[]{:S(2)}, u32[]{:S(2)}) collective-permute-start(bf16[3,128,512]{2,1,0:T(8,128)(2,1)S(1)} %chip_sum.17.refs_12_.refs_0_), channel_id=1, source_target_pairs={{0,8},{4,12},{24,16},{28,20},{1,9},{5,13},{25,17},{29,21},{2,10},{... | collective-permute-start | bytes 1179656 | tf_op jit(solution)/shard_map/ppermute | solution.py:251
  210.0 8.7 %collective-permute-done.35.refs_1_ = bf16[3,128,512]{2,1,0:T(8,128)(2,1)S(1)} collective-permute-done((bf16[3,128,512]{2,1,0:T(8,128)(2,1)S(1)}, bf16[3,128,512]{2,1,0:T(8,128)(2,1)S(1)}, u32[]{:S(2)}, u32[]{:S(2)}) %collective-permute-start.35) | collective-permute-done | bytes 393248 | tf_op jit(solution)/shard_map/ppermute | solution.py:251
  219.4 6.0 %backward_products.15 = (f32[256,1024]{1,0:T(8,128)S(1)}, f32[1024,256]{1,0:T(8,128)S(1)}, bf16[1024,6656]{1,0:T(8,128)(2,1)}, bf16[1024,6656]{1,0:T(8,128)(2,1)}, bf16[6656,1024]{1,0:T(8,128)(2,1)}) custom-call(bf16[3,128,768]{2,1,0:T(8,128)(2,1)S(1)} %choose.14.refs_2_.refs_0_, ...), custom_call_target="tpu_custom_call", output_to_operand_aliasing={{0}: (5, {}), {1}: (6, {}), {2}: (9, {}), {3}: (10, {}), {4... | custom-call | flops 1000 | bytes 1000 | tf_op jit(solution)/shard_map/backward_products/pallas_call | solution.py:46
  228.2 6.0 %backward_products.16 = (f32[256,1024]{1,0:T(8,128)S(1)}, f32[1024,256]{1,0:T(8,128)S(1)}, bf16[1024,6656]{1,0:T(8,128)(2,1)}, bf16[1024,6656]{1,0:T(8,128)(2,1)}, bf16[6656,1024]{1,0:T(8,128)(2,1)}) custom-call(bf16[3,128,768]{2,1,0:T(8,128)(2,1)S(1)} %choose.15.refs_2_.refs_0_, ...), custom_call_target="tpu_custom_call", output_to_operand_aliasing={{0}: (5, {}), {1}: (6, {}), {2}: (9, {}), {3}: (10, {}), {4... | custom-call | flops 1000 | bytes 1000 | tf_op jit(solution)/shard_map/backward_products/pallas_call | solution.py:46
  234.2 9.3 %collective-permute-done.47.refs_2_ = bf16[3,128,768]{2,1,0:T(8,128)(2,1)S(1)} collective-permute-done((bf16[3,128,768]{2,1,0:T(8,128)(2,1)S(1)}, bf16[3,128,768]{2,1,0:T(8,128)(2,1)S(1)}, u32[]{:S(2)}, u32[]{:S(2)}) %collective-permute-start.47) | collective-permute-done | bytes 589856 | tf_op jit(solution)/shard_map/ppermute | solution.py:268
  245.9 6.0 %backward_products.17 = (f32[256,1024]{1,0:T(8,128)S(1)}, f32[1024,256]{1,0:T(8,128)S(1)}, bf16[1024,6656]{1,0:T(8,128)(2,1)}, bf16[1024,6656]{1,0:T(8,128)(2,1)}, bf16[6656,1024]{1,0:T(8,128)(2,1)}) custom-call(bf16[3,128,768]{2,1,0:T(8,128)(2,1)S(1)} %choose.16.refs_0_.refs_12_, ...), custom_call_target="tpu_custom_call", output_to_operand_aliasing={{0}: (5, {}), {1}: (6, {}), {2}: (9, {}), {3}: (10, {}), {4... | custom-call | flops 1000 | bytes 1000 | tf_op jit(solution)/shard_map/backward_products/pallas_call | solution.py:46
  251.9 8.9 %collective-permute-done.46.refs_2_ = bf16[3,128,512]{2,1,0:T(8,128)(2,1)S(1)} collective-permute-done((bf16[3,128,512]{2,1,0:T(8,128)(2,1)S(1)}, bf16[3,128,512]{2,1,0:T(8,128)(2,1)S(1)}, u32[]{:S(2)}, u32[]{:S(2)}) %collective-permute-start.46) | collective-permute-done | bytes 393248 | tf_op jit(solution)/shard_map/ppermute | solution.py:268
  276.5 7.9 %collective-permute-done.51 = bf16[2,64,1024]{1,2,0:T(8,128)(2,1)S(1)} collective-permute-done((bf16[2,64,1024]{1,2,0:T(8,128)(2,1)S(1)}, bf16[2,64,1024]{1,2,0:T(8,128)(2,1)S(1)}, u32[]{:S(2)}, u32[]{:S(2)}) %collective-permute-start.51) | collective-permute-done | bytes 262176 | tf_op jit(solution)/shard_map/ppermute | solution.py:314
  284.4 12.2 %collective-permute-done.52 = bf16[2,64,1024]{1,2,0:T(8,128)(2,1)S(1)} collective-permute-done((bf16[2,64,1024]{1,2,0:T(8,128)(2,1)S(1)}, bf16[2,64,1024]{1,2,0:T(8,128)(2,1)S(1)}, u32[]{:S(2)}, u32[]{:S(2)}) %collective-permute-start.52) | collective-permute-done | bytes 262176 | tf_op jit(solution)/shard_map/ppermute | solution.py:314
  (195 shorter events, 139.7 us)
Async XLA Ops:
  38.0 24.6 %collective-permute-start.11 = (bf16[3,128,768]{2,1,0:T(8,128)(2,1)S(1)}, bf16[3,128,768]{2,1,0:T(8,128)(2,1)S(1)}, u32[]{:S(2)}, u32[]{:S(2)}) collective-permute-start(bf16[3,128,768]{2,1,0:T(8,128)(2,1)S(1)} %chip_sum.10.refs_5_.refs_0_), channel_id=1, source_target_pairs={{0,8},{4,12},{24,16},{28,20},{1,9},{5,13},{25,17},{29,21},{2,10},{... | collective-permute-start | bytes 1769480 | tf_op jit(solution)/shard_map/ppermute | solution.py:251
  48.1 18.3 %collective-permute-start.14 = (bf16[3,128,768]{2,1,0:T(8,128)(2,1)}, bf16[3,128,768]{2,1,0:T(8,128)(2,1)}, u32[]{:S(2)}, u32[]{:S(2)}) collective-permute-start(bf16[3,128,768]{2,1,0:T(8,128)(2,1)} %get-tuple-element.77), channel_id=1, source_target_pairs={{0,4},{4,0},{8,12},{12,8},{16,20},{20,16},{24,28},{28,24},{1,5},{5... | collective-permute-start | bytes 1769480 | tf_op jit(solution)/shard_map/ppermute | solution.py:245
  54.6 26.8 %collective-permute-start.13 = (bf16[3,128,768]{2,1,0:T(8,128)(2,1)}, bf16[3,128,768]{2,1,0:T(8,128)(2,1)}, u32[]{:S(2)}, u32[]{:S(2)}) collective-permute-start(bf16[3,128,768]{2,1,0:T(8,128)(2,1)} %chip_sum.11.refs_5_.refs_0_), channel_id=1, source_target_pairs={{0,8},{4,12},{24,16},{28,20},{1,9},{5,13},{25,17},{29,21},{2,10},{... | collective-permute-start | bytes 1769480 | tf_op jit(solution)/shard_map/ppermute | solution.py:251
  62.9 21.5 %collective-permute-start.12 = (bf16[3,128,768]{2,1,0:T(8,128)(2,1)S(1)}, bf16[3,128,768]{2,1,0:T(8,128)(2,1)}, u32[]{:S(2)}, u32[]{:S(2)}) collective-permute-start(bf16[3,128,768]{2,1,0:T(8,128)(2,1)S(1)} %half_sum.10.refs_2_.refs_0_), channel_id=1, source_target_pairs={{8,16},{12,20},{16,8},{20,12},{9,17},{13,21},{17,9},{21,13},{10,18... | collective-permute-start | bytes 1769480 | tf_op jit(solution)/shard_map/ppermute | solution.py:259
  64.4 22.9 %collective-permute-start.10 = (bf16[3,128,768]{2,1,0:T(8,128)(2,1)}, bf16[3,128,768]{2,1,0:T(8,128)(2,1)}, u32[]{:S(2)}, u32[]{:S(2)}) collective-permute-start(bf16[3,128,768]{2,1,0:T(8,128)(2,1)} %get-tuple-element.76), channel_id=1, source_target_pairs={{0,4},{4,0},{8,12},{12,8},{16,20},{20,16},{24,28},{28,24},{1,5},{5... | collective-permute-start | bytes 1769480 | tf_op jit(solution)/shard_map/ppermute | solution.py:245
  65.1 31.6 %collective-permute-start.18 = (bf16[3,128,768]{2,1,0:T(8,128)(2,1)S(1)}, bf16[3,128,768]{2,1,0:T(8,128)(2,1)}, u32[]{:S(2)}, u32[]{:S(2)}) collective-permute-start(bf16[3,128,768]{2,1,0:T(8,128)(2,1)S(1)} %activations.9.refs_2_.refs_0_), channel_id=1, source_target_pairs={{8,0},{12,4},{16,24},{20,28},{9,1},{13,5},{17,25},{21,29},{10,2},{... | collective-permute-start | bytes 1769480 | tf_op jit(solution)/shard_map/ppermute | solution.py:268
  75.2 27.4 %collective-permute-start.17 = (bf16[3,128,768]{2,1,0:T(8,128)(2,1)}, bf16[3,128,768]{2,1,0:T(8,128)(2,1)}, u32[]{:S(2)}, u32[]{:S(2)}) collective-permute-start(bf16[3,128,768]{2,1,0:T(8,128)(2,1)} %chip_sum.12.refs_5_.refs_0_), channel_id=1, source_target_pairs={{0,8},{4,12},{24,16},{28,20},{1,9},{5,13},{25,17},{29,21},{2,10},{... | collective-permute-start | bytes 1769480 | tf_op jit(solution)/shard_map/ppermute | solution.py:251
  90.2 20.1 %collective-permute-start.24 = (bf16[3,128,768]{2,1,0:T(8,128)(2,1)}, bf16[3,128,768]{2,1,0:T(8,128)(2,1)}, u32[]{:S(2)}, u32[]{:S(2)}) collective-permute-start(bf16[3,128,768]{2,1,0:T(8,128)(2,1)} %half_sum.11.refs_2_.refs_0_), channel_id=1, source_target_pairs={{8,16},{12,20},{16,8},{20,12},{9,17},{13,21},{17,9},{21,13},{10,18... | collective-permute-start | bytes 1769480 | tf_op jit(solution)/shard_map/ppermute | solution.py:259
  99.8 19.9 %collective-permute-start.22 = (bf16[3,128,768]{2,1,0:T(8,128)(2,1)}, bf16[3,128,768]{2,1,0:T(8,128)(2,1)S(1)}, u32[]{:S(2)}, u32[]{:S(2)}) collective-permute-start(bf16[3,128,768]{2,1,0:T(8,128)(2,1)} %choose.9.refs_2_.refs_0_), channel_id=1, source_target_pairs={{0,4},{4,0},{8,12},{12,8},{16,20},{20,16},{24,28},{28,24},{1,5},{5... | collective-permute-start | bytes 1769480 | tf_op jit(solution)/shard_map/ppermute | solution.py:279
  100.1 28.3 %collective-permute-start.21 = (bf16[3,128,768]{2,1,0:T(8,128)(2,1)}, bf16[3,128,768]{2,1,0:T(8,128)(2,1)}, u32[]{:S(2)}, u32[]{:S(2)}) collective-permute-start(bf16[3,128,768]{2,1,0:T(8,128)(2,1)} %activations.10.refs_2_.refs_0_), channel_id=1, source_target_pairs={{8,0},{12,4},{16,24},{20,28},{9,1},{13,5},{17,25},{21,29},{10,2},{... | collective-permute-start | bytes 1769480 | tf_op jit(solution)/shard_map/ppermute | solution.py:268
  102.6 29.8 %collective-permute-start.20 = (bf16[3,128,768]{2,1,0:T(8,128)(2,1)}, bf16[3,128,768]{2,1,0:T(8,128)(2,1)S(1)}, u32[]{:S(2)}, u32[]{:S(2)}) collective-permute-start(bf16[3,128,768]{2,1,0:T(8,128)(2,1)} %chip_sum.13.refs_5_.refs_0_), channel_id=1, source_target_pairs={{0,8},{4,12},{24,16},{28,20},{1,9},{5,13},{25,17},{29,21},{2,10},{... | collective-permute-start | bytes 1769480 | tf_op jit(solution)/shard_map/ppermute | solution.py:251
  110.3 29.4 %collective-permute-start.16 = (bf16[3,128,768]{2,1,0:T(8,128)(2,1)}, bf16[3,128,768]{2,1,0:T(8,128)(2,1)S(1)}, u32[]{:S(2)}, u32[]{:S(2)}) collective-permute-start(bf16[3,128,768]{2,1,0:T(8,128)(2,1)} %copy-done.16), channel_id=1, source_target_pairs={{0,4},{4,0},{8,12},{12,8},{16,20},{20,16},{24,28},{28,24},{1,5},{5... | collective-permute-start | bytes 1769480 | tf_op jit(solution)/shard_map/ppermute | solution.py:245
  114.7 24.3 %collective-permute-start.19 = (bf16[3,128,768]{2,1,0:T(8,128)(2,1)S(1)}, bf16[3,128,768]{2,1,0:T(8,128)(2,1)S(1)}, u32[]{:S(2)}, u32[]{:S(2)}) collective-permute-start(bf16[3,128,768]{2,1,0:T(8,128)(2,1)S(1)} %half_sum.12.refs_2_.refs_0_), channel_id=1, source_target_pairs={{8,16},{12,20},{16,8},{20,12},{9,17},{13,21},{17,9},{21,13},{10,18... | collective-permute-start | bytes 1769480 | tf_op jit(solution)/shard_map/ppermute | solution.py:259
  131.1 18.7 %collective-permute-start.27 = (bf16[3,128,768]{2,1,0:T(8,128)(2,1)S(1)}, bf16[3,128,768]{2,1,0:T(8,128)(2,1)S(1)}, u32[]{:S(2)}, u32[]{:S(2)}) collective-permute-start(bf16[3,128,768]{2,1,0:T(8,128)(2,1)S(1)} %activations.11.refs_2_.refs_0_), channel_id=1, source_target_pairs={{8,0},{12,4},{16,24},{20,28},{9,1},{13,5},{17,25},{21,29},{10,2},{... | collective-permute-start | bytes 1769480 | tf_op jit(solution)/shard_map/ppermute | solution.py:268
  132.4 19.5 %collective-permute-start.26 = (bf16[3,128,768]{2,1,0:T(8,128)(2,1)S(1)}, bf16[3,128,768]{2,1,0:T(8,128)(2,1)S(1)}, u32[]{:S(2)}, u32[]{:S(2)}) collective-permute-start(bf16[3,128,768]{2,1,0:T(8,128)(2,1)S(1)} %chip_sum.14.refs_5_.refs_0_), channel_id=1, source_target_pairs={{0,8},{4,12},{24,16},{28,20},{1,9},{5,13},{25,17},{29,21},{2,10},{... | collective-permute-start | bytes 1769480 | tf_op jit(solution)/shard_map/ppermute | solution.py:251
  139.1 19.1 %collective-permute-start.33 = (bf16[3,128,768]{2,1,0:T(8,128)(2,1)S(1)}, bf16[3,128,768]{2,1,0:T(8,128)(2,1)S(1)}, u32[]{:S(2)}, u32[]{:S(2)}) collective-permute-start(bf16[3,128,768]{2,1,0:T(8,128)(2,1)S(1)} %get-tuple-element.95), channel_id=1, source_target_pairs={{0,4},{4,0},{8,12},{12,8},{16,20},{20,16},{24,28},{28,24},{1,5},{5... | collective-permute-start | bytes 1769480 | tf_op jit(solution)/shard_map/ppermute | solution.py:245
  151.9 18.1 %collective-permute-start.30 = (bf16[3,128,768]{2,1,0:T(8,128)(2,1)S(1)}, bf16[3,128,768]{2,1,0:T(8,128)(2,1)S(1)}, u32[]{:S(2)}, u32[]{:S(2)}) collective-permute-start(bf16[3,128,768]{2,1,0:T(8,128)(2,1)S(1)} %chip_sum.15.refs_5_.refs_0_), channel_id=1, source_target_pairs={{0,8},{4,12},{24,16},{28,20},{1,9},{5,13},{25,17},{29,21},{2,10},{... | collective-permute-start | bytes 1769480 | tf_op jit(solution)/shard_map/ppermute | solution.py:251
  156.9 17.8 %collective-permute-start.29 = (bf16[3,128,768]{2,1,0:T(8,128)(2,1)S(1)}, bf16[3,128,768]{2,1,0:T(8,128)(2,1)S(1)}, u32[]{:S(2)}, u32[]{:S(2)}) collective-permute-start(bf16[3,128,768]{2,1,0:T(8,128)(2,1)S(1)} %half_sum.14.refs_2_.refs_0_), channel_id=1, source_target_pairs={{8,16},{12,20},{16,8},{20,12},{9,17},{13,21},{17,9},{21,13},{10,18... | collective-permute-start | bytes 1769480 | tf_op jit(solution)/shard_map/ppermute | solution.py:259
  168.1 17.6 %collective-permute-start.37 = (bf16[3,128,768]{2,1,0:T(8,128)(2,1)S(1)}, bf16[3,128,768]{2,1,0:T(8,128)(2,1)S(1)}, u32[]{:S(2)}, u32[]{:S(2)}) collective-permute-start(bf16[3,128,768]{2,1,0:T(8,128)(2,1)S(1)} %activations.13.refs_2_.refs_0_), channel_id=1, source_target_pairs={{8,0},{12,4},{16,24},{20,28},{9,1},{13,5},{17,25},{21,29},{10,2},{... | collective-permute-start | bytes 1769480 | tf_op jit(solution)/shard_map/ppermute | solution.py:268
  187.8 31.2 %collective-permute-start.45 = (bf16[3,128,768]{2,1,0:T(8,128)(2,1)S(1)}, bf16[3,128,768]{2,1,0:T(8,128)(2,1)S(1)}, u32[]{:S(2)}, u32[]{:S(2)}) collective-permute-start(bf16[3,128,768]{2,1,0:T(8,128)(2,1)S(1)} %half_sum.16.refs_2_.refs_0_), channel_id=1, source_target_pairs={{8,16},{12,20},{16,8},{20,12},{9,17},{13,21},{17,9},{21,13},{10,18... | collective-permute-start | bytes 1769480 | tf_op jit(solution)/shard_map/ppermute | solution.py:259
  204.1 21.4 %collective-permute-start.43 = (bf16[3,128,768]{2,1,0:T(8,128)(2,1)S(1)}, bf16[3,128,768]{2,1,0:T(8,128)(2,1)S(1)}, u32[]{:S(2)}, u32[]{:S(2)}) collective-permute-start(bf16[3,128,768]{2,1,0:T(8,128)(2,1)S(1)} %activations.15.refs_12_.refs_0_), channel_id=1, source_target_pairs={{8,0},{12,4},{16,24},{20,28},{9,1},{13,5},{17,25},{21,29},{10,2},{... | collective-permute-start | bytes 1769480 | tf_op jit(solution)/shard_map/ppermute | solution.py:268
  225.8 17.7 %collective-permute-start.47 = (bf16[3,128,768]{2,1,0:T(8,128)(2,1)S(1)}, bf16[3,128,768]{2,1,0:T(8,128)(2,1)S(1)}, u32[]{:S(2)}, u32[]{:S(2)}) collective-permute-start(bf16[3,128,768]{2,1,0:T(8,128)(2,1)S(1)} %activations.16.refs_12_.refs_0_), channel_id=1, source_target_pairs={{8,0},{12,4},{16,24},{20,28},{9,1},{13,5},{17,25},{21,29},{10,2},{... | collective-permute-start | bytes 1769480 | tf_op jit(solution)/shard_map/ppermute | solution.py:268
  271.7 24.9 %collective-permute-start.52 = (bf16[2,64,1024]{1,2,0:T(8,128)(2,1)S(1)}, bf16[2,64,1024]{1,2,0:T(8,128)(2,1)S(1)}, u32[]{:S(2)}, u32[]{:S(2)}) collective-permute-start(bf16[2,64,1024]{1,2,0:T(8,128)(2,1)S(1)} %get-tuple-element.138), channel_id=1, source_target_pairs={{0,2},{1,3},{2,0},{3,1},{4,6},{5,7},{6,4},{7,5},{8,10},{9,11},{10,... | collective-permute-start | bytes 786440 | tf_op jit(solution)/shard_map/ppermute | solution.py:314
  273.2 23.4 %collective-permute-start.53 = (bf16[2,64,1024]{1,2,0:T(8,128)(2,1)S(1)}, bf16[2,64,1024]{1,2,0:T(8,128)(2,1)S(1)}, u32[]{:S(2)}, u32[]{:S(2)}) collective-permute-start(bf16[2,64,1024]{1,2,0:T(8,128)(2,1)S(1)} %get-tuple-element.137), channel_id=1, source_target_pairs={{0,3},{1,2},{2,1},{3,0},{4,7},{5,6},{6,5},{7,4},{8,11},{9,10},{10,... | collective-permute-start | bytes 786440 | tf_op jit(solution)/shard_map/ppermute | solution.py:314
  (47 other events, 650.0 us)
where the time goes:
time: 301 us; the launch traced here: 298 us
  Pallas kernels  128 us (43%)
  starting transfers between devices  79.8 us (27%)
  waiting for transfers between devices  73.7 us (24%)
  local copies, waits for them, and re-layouts  11.2 us (4%)
  other arithmetic  4.02 us (1%)
    pallas_call x55, Pallas kernels, call(): pl.pallas_call(body, grid=grid, in_specs=list(in_specs) + [ANYWHERE] * le...  128 us
    ppermute x9, starting transfers between devices, step_chip(): arrived[k] = lax.ppermute(partial[k], 'row', inward[0])  42.5 us
    ppermute x9, waiting for transfers between devices, step_act(): arrived[k] = lax.ppermute(acts[k], 'row', back)  33.7 us
    ppermute x3, waiting for transfers between devices, shards(): lax.ppermute(piece, 'col', [(s, s ^ j) for s in range(n_col)]).astype(F32)  20.1 us
    ppermute x9, starting transfers between devices, step_act(): arrived[k] = lax.ppermute(acts[k], 'row', back)  11.8 us
    ppermute x9, waiting for transfers between devices, step_chip(): arrived[k] = lax.ppermute(partial[k], 'row', inward[0])  11.6 us
    ppermute x6, starting transfers between devices, gather(): lax.ppermute(block, 'col', [(s, s ^ j) for s in range(n_col)])  10.3 us
    unnamed x40, local copies, waits for them, and re-layouts  8.23 us
  transfers between devices with their start and end apart: 54, of which 13 were waited for; matrix products, arithmetic and copies ran while one was open for 1% of the time, Pallas kernels for 40%

commit v1 on v0

--- a/solution.py
+++ b/solution.py
@@ -10,8 +10,7 @@
 F32 = jnp.float32
 BF16 = jnp.bfloat16
 MOST_CHUNKS = 9
-PRODUCT_VMEM = 40 * 1024 * 1024
-SMALL_VMEM = 10 * 1024 * 1024
+KERNEL_VMEM = 42 * 1024 * 1024
 ANYWHERE = pl.BlockSpec(memory_space=pl.ANY)
 
 
@@ -29,6 +28,10 @@
     return 256 if width % 256 == 0 else 128
 
 
+def contract_last(left, right):
+    return lax.dot_general(left, right, (((1,), (1,)), ((), ())), preferred_element_type=F32)
+
+
 def whole(shape):
     return pl.BlockSpec(shape, lambda i: (0,) * len(shape))
 
@@ -38,7 +41,7 @@
         self.last = None
 
     def call(self, kernel, grid, in_specs, out_specs, out_shape, aliases, vmem, cost, name, *args):
-        extra = [] if self.last is None else [self.last]
+        extra = [] if self.last is None or any(self.last is a for a in args) else [self.last]
 
         def body(*refs):
             kernel(*refs[: len(args)], *refs[len(args) + len(extra) :])
@@ -58,19 +61,19 @@
         return out
 
 
-def forward_kernel(x_ref, ct_ref, gate_ref, up_ref, down_ref, mine_ref, theirs_ref):
+def forward_kernel(x_ref, c_ref, gate_ref, up_ref, down_ref, mine_ref, theirs_ref):
     half = mine_ref.shape[1]
     sums = (
         jnp.dot(x_ref[...], gate_ref[...], preferred_element_type=F32),
         jnp.dot(x_ref[...], up_ref[...], preferred_element_type=F32),
-        jnp.dot(down_ref[...], ct_ref[...], preferred_element_type=F32).T,
+        contract_last(c_ref[...], down_ref[...]),
     )
     for index, value in enumerate(sums):
         mine_ref[index] = value[:half].astype(BF16)
         theirs_ref[index] = value[half:].astype(BF16)
 
 
-def forward(order, x, ct, gate, up, down, start, width):
+def forward(order, x, c, gate, up, down, start, width):
     tokens, depth = x.shape
     tile = tile_of(width)
     first = start // tile
@@ -82,25 +85,23 @@
     return order.call(
         forward_kernel,
         (width // tile,),
-        [whole(x.shape), whole(ct.shape), column, column, row],
+        [whole(x.shape), whole(c.shape), column, column, row],
         [piece, piece],
         [part, part],
         {},
-        PRODUCT_VMEM,
+        KERNEL_VMEM,
         1000,
         "forward_sums",
-        x, ct, gate, up, down,
+        x, c, gate, up, down,
     )
 
 
 def elementwise(order, kernel, name, *args):
-    _, half, width = args[0].shape
-    tile = tile_of(width)
-    piece = pl.BlockSpec((3, half, tile), lambda i: (0, 0, i))
+    piece = whole(args[0].shape)
     specs = [piece if a.ndim == 3 else pl.BlockSpec(memory_space=pltpu.SMEM) for a in args]
     shape = jax.ShapeDtypeStruct(args[0].shape, BF16)
     return order.call(
-        kernel, (width // tile,), specs, [piece], [shape], {}, SMALL_VMEM, 1000, name, *args
+        kernel, (1,), specs, [piece], [shape], {}, KERNEL_VMEM, 1000, name, *args
     )[0]
 
 
@@ -133,20 +134,17 @@
     return [jnp.concatenate([mine_ref[i], other_ref[i]], axis=0) for i in range(3)]
 
 
-def token_products(acts, weight_refs, before_refs, mixed_ref, inputs_ref):
+def token_products(acts, weight_refs, before_refs, total_ref):
     gate_ref, up_ref, down_ref = weight_refs
+    hidden, gate_act, up_act = acts
 
     @pl.when(pl.program_id(0) == 0)
     def _():
         if not before_refs:
-            mixed_ref[...] = jnp.zeros_like(mixed_ref)
-            inputs_ref[...] = jnp.zeros_like(inputs_ref)
-
-    hidden, gate_act, up_act = acts
-    mixed_ref[...] += jnp.dot(hidden, down_ref[...], preferred_element_type=F32)
-    inputs_ref[...] += jnp.dot(
-        gate_ref[...], gate_act.T, preferred_element_type=F32
-    ) + jnp.dot(up_ref[...], up_act.T, preferred_element_type=F32)
+            total_ref[...] = jnp.zeros_like(total_ref)
+
+    total_ref[0] += jnp.dot(hidden, down_ref[...], preferred_element_type=F32)
+    total_ref[1] += contract_last(gate_act, gate_ref[...]) + contract_last(up_act, up_ref[...])
 
 
 def weight_products(acts, xt_ref, c_ref, grad_gate_ref, grad_up_ref, grad_down_ref):
@@ -156,7 +154,7 @@
     grad_down_ref[...] = jnp.dot(hidden.T, c_ref[...], preferred_element_type=F32).astype(BF16)
 
 
-def backward(order, mine, other, xt, c, weights, start, totals, grads, parts):
+def backward(order, mine, other, xt, c, weights, start, total, grads, parts):
     _, half, width = mine.shape
     tile = tile_of(width)
     first = start // tile
@@ -169,12 +167,12 @@
     if with_tokens:
         specs += [column, column, row]
         args += weights
-        for index, total in enumerate(totals or ()):
-            aliases[len(args)] = index
+        if total is not None:
+            aliases[len(args)] = 0
             specs += [resident]
             args += [total]
-        out_specs += [resident, resident]
-        shapes += [jax.ShapeDtypeStruct(a.shape, F32) for a in (c, xt)]
+        out_specs += [resident]
+        shapes += [jax.ShapeDtypeStruct((2,) + c.shape, F32)]
     n_token_args = len(args)
     if with_weights:
         specs += [whole(xt.shape), whole(c.shape)]
@@ -190,15 +188,15 @@
         ins, outs = refs[: len(args)], refs[len(args) :]
         acts = joined(*ins[:2])
         if with_tokens:
-            token_products(acts, ins[2:5], ins[5:n_token_args], *outs[:2])
+            token_products(acts, ins[2:5], ins[5:n_token_args], outs[0])
         if with_weights:
             weight_products(acts, *ins[n_token_args : n_token_args + 2], *outs[-3:])
 
     out = order.call(
-        kernel, (width // tile,), specs, out_specs, shapes, aliases, PRODUCT_VMEM, 1000,
+        kernel, (width // tile,), specs, out_specs, shapes, aliases, KERNEL_VMEM, 1000,
         "backward_products", *args,
     )
-    return (out[:2] if with_tokens else totals), (out[-3:] if with_weights else grads)
+    return (out[0] if with_tokens else total), (out[-3:] if with_weights else grads)
 
 
 def both_cores(pairs):
@@ -231,7 +229,7 @@
 
     x = gather(tokens)
     c = gather(cotangent)
-    xt, ct = x.T, c.T
+    xt = x.T
 
     order = Order()
     chunks = chunks_of(gate_weight.shape[1])
@@ -241,7 +239,7 @@
 
     def step_sums(k):
         if 0 <= k < count:
-            mine, theirs = forward(order, x, ct, *weights, *chunks[k])
+            mine, theirs = forward(order, x, c, *weights, *chunks[k])
             swapped[k] = (mine, lax.ppermute(theirs, "row", siblings))
 
     def step_chip(k):
@@ -287,20 +285,29 @@
     step_sums(0)
     step_sums(1)
     step_chip(0)
-    step_sums(2)
     step_chip(1)
-    step_sums(3)
-    for k in range(count + 2):
+    summed = 2
+    deferred = [k for k in range(count - 6, count - 3) if k >= 0] + [count - 1]
+    for k in range(count):
+        fresh = range(summed, min(count, summed + (3 if k == 0 else 2)))
+        summed = fresh.stop
+        for j in fresh:
+            step_sums(j)
         step_half(k)
         step_act(k - 1)
-        step_chip(k + 2)
-        step_sums(k + 4)
-        if k - 3 < count - 1:
-            step_back(k - 3)
         step_choose(k - 2)
+        for j in fresh:
+            step_chip(j)
+        step_back(k - 3, ("tokens",) if k - 3 in deferred else ("tokens", "weights"))
+    for k in deferred[:2]:
+        step_back(k, ("weights",))
+    step_act(count - 1)
+    step_choose(count - 2)
+    step_back(count - 3)
+    step_back(count - 2)
+    step_choose(count - 1)
     step_back(count - 1, ("tokens",))
-    mixed, inputs = state[0]
-    total = jnp.stack([mixed, inputs.T])
+    total = state[0]
 
     half = total.shape[1] // 2
     block = total.shape[1] // n_col
@@ -313,7 +320,8 @@
         piece = ordered[:, j * block : (j + 1) * block]
         out += lax.ppermute(piece, "col", [(s, s ^ j) for s in range(n_col)]).astype(F32)
     out = out.astype(BF16)
-    step_back(count - 1, ("weights",))
+    for k in deferred[2:]:
+        step_back(k, ("weights",))
     return out[0], out[1], *state[1]
 
 

time: 301 us -> 239 us (0.79)
  waiting for transfers between devices: 73.7 us -> 30 us
  Pallas kernels: 128 us -> 112 us
    ppermute x9, waiting for transfers between devices: 33.7 us -> 14 us  [step_act(): arrived[k] = lax.ppermute(acts[k], 'row', back)]
    pallas_call x55 -> x58, Pallas kernels: 128 us -> 112 us  [call(): pl.pallas_call(body, grid=grid, in_specs=list(in_specs) + [ANYWHERE] * le...]
    ppermute x3, waiting for transfers between devices: 20.1 us -> 6.87 us  [shards(): lax.ppermute(piece, 'col', [(s, s ^ j) for s in range(n_col)]).astype(F32)]
    ppermute x9, waiting for transfers between devices: 11.6 us -> 0.14 us  [step_chip(): arrived[k] = lax.ppermute(partial[k], 'row', inward[0])]
  transfers between devices with their start and end apart: 54 -> 54, of which waited for: 13 -> 12; matrix products, arithmetic and copies ran while one was open for 1% -> 1% of each run, Pallas kernels for 40% -> 45%
where the time goes in v1:
time: 239 us; the launch traced here: 236 us
  Pallas kernels  112 us (47%)
  starting transfers between devices  79.8 us (33%)
  waiting for transfers between devices  30 us (13%)
  local copies, waits for them, and re-layouts  11 us (5%)
    pallas_call x58, Pallas kernels, call(): pl.pallas_call(body, grid=grid, in_specs=list(in_specs) + [ANYWHERE] * le...  112 us
    ppermute x9, starting transfers between devices, step_chip(): arrived[k] = lax.ppermute(partial[k], 'row', inward[0])  42.2 us
    ppermute x9, waiting for transfers between devices, step_act(): arrived[k] = lax.ppermute(acts[k], 'row', back)  14 us
    ppermute x9, starting transfers between devices, step_act(): arrived[k] = lax.ppermute(acts[k], 'row', back)  11.8 us
    ppermute x6, starting transfers between devices, gather(): lax.ppermute(block, 'col', [(s, s ^ j) for s in range(n_col)])  10.3 us
    unnamed x40, local copies, waits for them, and re-layouts  8.8 us
    ppermute x9, starting transfers between devices, step_half(): arrived[k] = lax.ppermute(partial[k], 'row', across)  7.84 us
    ppermute x3, waiting for transfers between devices, shards(): lax.ppermute(piece, 'col', [(s, s ^ j) for s in range(n_col)]).astype(F32)  6.87 us
  transfers between devices with their start and end apart: 54, of which 12 were waited for; matrix products, arithmetic and copies ran while one was open for 1% of the time, Pallas kernels for 45%

profile of v1, /device:TPU:0, one launch (start us, length us, event | category | flops | bytes accessed | tf_op | source)
XLA Modules:
  0.0 236.5 jit_solution(17653913518935349835)
XLA Ops:
  24.2 4.0 %forward_sums.10 = (bf16[3,128,768]{2,1,0:T(8,128)(2,1)S(1)}, bf16[3,128,768]{2,1,0:T(8,128)(2,1)S(1)}) custom-call(bf16[256,1024]{1,0:T(8,128)(2,1)S(1)} %get-tuple-element.111.refs_0_, bf16[256,1024]{1,0:T(8,128)(2,1)S(1)} %pad_maximum_fusion.1.refs_1_.refs_6_.refs_7_.refs_3_, bf16[1024,6656]{1,0:T(8,128)(2,1)} %refs_2_.35, bf16[1024,6656]{1,0:T(8,128)(2,1)} %refs_3_.35, ...), custom_call_target="tpu_custom_call" | custom-call | flops 1000 | bytes 1000 | tf_op jit(solution)/shard_map/forward_sums/pallas_call | solution.py:49
  34.0 4.0 %forward_sums.11 = (bf16[3,128,768]{2,1,0:T(8,128)(2,1)S(1)}, bf16[3,128,768]{2,1,0:T(8,128)(2,1)S(1)}) custom-call(bf16[256,1024]{1,0:T(8,128)(2,1)S(1)} %get-tuple-element.111.refs_0_, bf16[256,1024]{1,0:T(8,128)(2,1)S(1)} %pad_maximum_fusion.1.refs_1_.refs_6_.refs_7_.refs_3_, bf16[1024,6656]{1,0:T(8,128)(2,1)} %refs_2_.35, bf16[1024,6656]{1,0:T(8,128)(2,1)} %refs_3_.35, ...), custom_call_target="tpu_custom_call" | custom-call | flops 1000 | bytes 1000 | tf_op jit(solution)/shard_map/forward_sums/pallas_call | solution.py:49
  38.0 4.0 %forward_sums.12 = (bf16[3,128,768]{2,1,0:T(8,128)(2,1)S(1)}, bf16[3,128,768]{2,1,0:T(8,128)(2,1)S(1)}) custom-call(bf16[256,1024]{1,0:T(8,128)(2,1)S(1)} %get-tuple-element.111.refs_0_, bf16[256,1024]{1,0:T(8,128)(2,1)S(1)} %pad_maximum_fusion.1.refs_1_.refs_6_.refs_7_.refs_3_, bf16[1024,6656]{1,0:T(8,128)(2,1)} %refs_2_.35, bf16[1024,6656]{1,0:T(8,128)(2,1)} %refs_3_.35, ...), custom_call_target="tpu_custom_call" | custom-call | flops 1000 | bytes 1000 | tf_op jit(solution)/shard_map/forward_sums/pallas_call | solution.py:49
  42.6 4.0 %forward_sums.13 = (bf16[3,128,768]{2,1,0:T(8,128)(2,1)S(1)}, bf16[3,128,768]{2,1,0:T(8,128)(2,1)S(1)}) custom-call(bf16[256,1024]{1,0:T(8,128)(2,1)S(1)} %get-tuple-element.111.refs_0_, bf16[256,1024]{1,0:T(8,128)(2,1)S(1)} %pad_maximum_fusion.1.refs_1_.refs_6_.refs_7_.refs_3_, bf16[1024,6656]{1,0:T(8,128)(2,1)} %refs_2_.35, bf16[1024,6656]{1,0:T(8,128)(2,1)} %refs_3_.35, ...), custom_call_target="tpu_custom_call" | custom-call | flops 1000 | bytes 1000 | tf_op jit(solution)/shard_map/forward_sums/pallas_call | solution.py:49
  49.7 4.0 %forward_sums.14 = (bf16[3,128,768]{2,1,0:T(8,128)(2,1)S(1)}, bf16[3,128,768]{2,1,0:T(8,128)(2,1)S(1)}) custom-call(bf16[256,1024]{1,0:T(8,128)(2,1)S(1)} %get-tuple-element.111.refs_0_, bf16[256,1024]{1,0:T(8,128)(2,1)S(1)} %pad_maximum_fusion.1.refs_1_.refs_6_.refs_7_.refs_3_, bf16[1024,6656]{1,0:T(8,128)(2,1)} %refs_2_.35, bf16[1024,6656]{1,0:T(8,128)(2,1)} %refs_3_.35, ...), custom_call_target="tpu_custom_call" | custom-call | flops 1000 | bytes 1000 | tf_op jit(solution)/shard_map/forward_sums/pallas_call | solution.py:49
  54.0 4.0 %forward_sums.15 = (bf16[3,128,768]{2,1,0:T(8,128)(2,1)S(1)}, bf16[3,128,768]{2,1,0:T(8,128)(2,1)S(1)}) custom-call(bf16[256,1024]{1,0:T(8,128)(2,1)S(1)} %get-tuple-element.111.refs_0_, bf16[256,1024]{1,0:T(8,128)(2,1)S(1)} %pad_maximum_fusion.1.refs_1_.refs_6_.refs_7_.refs_3_, bf16[1024,6656]{1,0:T(8,128)(2,1)} %refs_2_.35, bf16[1024,6656]{1,0:T(8,128)(2,1)} %refs_3_.35, ...), custom_call_target="tpu_custom_call" | custom-call | flops 1000 | bytes 1000 | tf_op jit(solution)/shard_map/forward_sums/pallas_call | solution.py:49
  58.3 5.9 %collective-permute-start.20 = (bf16[3,128,768]{2,1,0:T(8,128)(2,1)S(1)}, bf16[3,128,768]{2,1,0:T(8,128)(2,1)S(1)}, u32[]{:S(2)}, u32[]{:S(2)}) collective-permute-start(bf16[3,128,768]{2,1,0:T(8,128)(2,1)S(1)} %chip_sum.11.refs_2_.refs_0_), channel_id=1, source_target_pairs={{0,8},{4,12},{24,16},{28,20},{1,9},{5,13},{25,17},{29,21},{2,10},{... | collective-permute-start | bytes 1769480 | tf_op jit(solution)/shard_map/ppermute | solution.py:249
  67.1 4.9 %forward_sums.16 = (bf16[3,128,768]{2,1,0:T(8,128)(2,1)S(1)}, bf16[3,128,768]{2,1,0:T(8,128)(2,1)}) custom-call(bf16[256,1024]{1,0:T(8,128)(2,1)S(1)} %get-tuple-element.111.refs_0_, bf16[256,1024]{1,0:T(8,128)(2,1)S(1)} %pad_maximum_fusion.1.refs_1_.refs_6_.refs_7_.refs_3_, bf16[1024,6656]{1,0:T(8,128)(2,1)} %refs_2_.35, bf16[1024,6656]{1,0:T(8,128)(2,1)} %refs_3_.35, ...), custom_call_target="tpu_custom_call" | custom-call | flops 1000 | bytes 1000 | tf_op jit(solution)/shard_map/forward_sums/pallas_call | solution.py:49
  72.1 6.2 %collective-permute-start.26 = (bf16[3,128,768]{2,1,0:T(8,128)(2,1)S(1)}, bf16[3,128,768]{2,1,0:T(8,128)(2,1)}, u32[]{:S(2)}, u32[]{:S(2)}) collective-permute-start(bf16[3,128,768]{2,1,0:T(8,128)(2,1)S(1)} %chip_sum.12.refs_2_.refs_0_), channel_id=1, source_target_pairs={{0,8},{4,12},{24,16},{28,20},{1,9},{5,13},{25,17},{29,21},{2,10},{... | collective-permute-start | bytes 1769480 | tf_op jit(solution)/shard_map/ppermute | solution.py:249
  91.5 6.0 %collective-permute-start.22 = (bf16[3,128,768]{2,1,0:T(8,128)(2,1)}, bf16[3,128,768]{2,1,0:T(8,128)(2,1)}, u32[]{:S(2)}, u32[]{:S(2)}) collective-permute-start(bf16[3,128,768]{2,1,0:T(8,128)(2,1)} %copy-done.6), channel_id=1, source_target_pairs={{0,8},{4,12},{24,16},{28,20},{1,9},{5,13},{25,17},{29,21},{2,10},{... | collective-permute-start | bytes 1769480 | tf_op jit(solution)/shard_map/ppermute | solution.py:249
  108.3 6.1 %collective-permute-start.28 = (bf16[3,128,768]{2,1,0:T(8,128)(2,1)}, bf16[3,128,768]{2,1,0:T(8,128)(2,1)}, u32[]{:S(2)}, u32[]{:S(2)}) collective-permute-start(bf16[3,128,768]{2,1,0:T(8,128)(2,1)} %copy-done), channel_id=1, source_target_pairs={{0,8},{4,12},{24,16},{28,20},{1,9},{5,13},{25,17},{29,21},{2,10},{... | collective-permute-start | bytes 1769480 | tf_op jit(solution)/shard_map/ppermute | solution.py:249
  117.8 6.5 %backward_products.13 = (f32[2,256,1024]{2,1,0:T(8,128)S(1)}, bf16[1024,6656]{1,0:T(8,128)(2,1)}, bf16[1024,6656]{1,0:T(8,128)(2,1)}, bf16[6656,1024]{1,0:T(8,128)(2,1)}) custom-call(bf16[3,128,768]{2,1,0:T(8,128)(2,1)S(1)} %copy-done.3, bf16[3,128,768]{2,1,0:T(8,128)(2,1)S(1)} %copy-done.17, bf16[1024,6656]{1,0:T(8,128)(2,1)} %refs_2_.35, ...), custom_call_target="tpu_custom_call" | custom-call | flops 1000 | bytes 1000 | tf_op jit(solution)/shard_map/backward_products/pallas_call | solution.py:49
  130.4 4.4 %collective-permute-start.34 = (bf16[3,128,768]{2,1,0:T(8,128)(2,1)S(1)}, bf16[3,128,768]{2,1,0:T(8,128)(2,1)S(1)}, u32[]{:S(2)}, u32[]{:S(2)}) collective-permute-start(bf16[3,128,768]{2,1,0:T(8,128)(2,1)S(1)} %copy-done.5), channel_id=1, source_target_pairs={{0,8},{4,12},{24,16},{28,20},{1,9},{5,13},{25,17},{29,21},{2,10},{... | collective-permute-start | bytes 1769480 | tf_op jit(solution)/shard_map/ppermute | solution.py:249
  134.9 6.3 %backward_products.14 = (f32[2,256,1024]{2,1,0:T(8,128)S(1)}, bf16[1024,6656]{1,0:T(8,128)(2,1)}, bf16[1024,6656]{1,0:T(8,128)(2,1)}, bf16[6656,1024]{1,0:T(8,128)(2,1)}) custom-call(bf16[3,128,768]{2,1,0:T(8,128)(2,1)S(1)} %choose.10.refs_7_.refs_0_, ...), custom_call_target="tpu_custom_call", output_to_operand_aliasing={{0}: (5, {}), {1}: (8, {}), {2}: (9, {}), {3}: (10, {})} | custom-call | flops 1000 | bytes 1000 | tf_op jit(solution)/shard_map/backward_products/pallas_call | solution.py:49
  145.2 4.3 %collective-permute-start.41 = (bf16[3,128,768]{2,1,0:T(8,128)(2,1)S(1)}, bf16[3,128,768]{2,1,0:T(8,128)(2,1)S(1)}, u32[]{:S(2)}, u32[]{:S(2)}) collective-permute-start(bf16[3,128,768]{2,1,0:T(8,128)(2,1)S(1)} %chip_sum.16.refs_2_.refs_0_), channel_id=1, source_target_pairs={{0,8},{4,12},{24,16},{28,20},{1,9},{5,13},{25,17},{29,21},{2,10},{... | collective-permute-start | bytes 1769480 | tf_op jit(solution)/shard_map/ppermute | solution.py:249
  149.5 6.2 %backward_products.15 = (f32[2,256,1024]{2,1,0:T(8,128)S(1)}, bf16[1024,6656]{1,0:T(8,128)(2,1)}, bf16[1024,6656]{1,0:T(8,128)(2,1)}, bf16[6656,1024]{1,0:T(8,128)(2,1)}) custom-call(bf16[3,128,768]{2,1,0:T(8,128)(2,1)S(1)} %choose.11.refs_11_.refs_0_, ...), custom_call_target="tpu_custom_call", output_to_operand_aliasing={{0}: (5, {}), {1}: (8, {}), {2}: (9, {}), {3}: (10, {})} | custom-call | flops 1000 | bytes 1000 | tf_op jit(solution)/shard_map/backward_products/pallas_call | solution.py:49
  160.9 4.0 %backward_products.16.refs_2_.refs_5_ = f32[2,256,1024]{2,1,0:T(8,128)S(1)} custom-call(bf16[3,128,768]{2,1,0:T(8,128)(2,1)S(1)} %choose.12.refs_11_.refs_0_, bf16[3,128,768]{2,1,0:T(8,128)(2,1)S(1)} %collective-permute-done.38.refs_1_, bf16[1024,6656]{1,0:T(8,128)(2,1)} %refs_2_.35, bf16[1024,6656]{1,0:T(8,128)(2,1)} %refs_3_.35, ...), custom_call_target="tpu_custom_call", output_to_operand_aliasing={{}: (5, {})} | custom-call | flops 1000 | bytes 1000 | tf_op jit(solution)/shard_map/backward_products/pallas_call | solution.py:49
  165.8 4.0 %collective-permute-start.21 = (bf16[3,128,512]{2,1,0:T(8,128)(2,1)S(1)}, bf16[3,128,512]{2,1,0:T(8,128)(2,1)S(1)}, u32[]{:S(2)}, u32[]{:S(2)}) collective-permute-start(bf16[3,128,512]{2,1,0:T(8,128)(2,1)S(1)} %copy-done.9), channel_id=1, source_target_pairs={{0,8},{4,12},{24,16},{28,20},{1,9},{5,13},{25,17},{29,21},{2,10},{... | collective-permute-start | bytes 1179656 | tf_op jit(solution)/shard_map/ppermute | solution.py:249
  174.4 4.0 %backward_products.17.refs_2_.refs_5_ = f32[2,256,1024]{2,1,0:T(8,128)S(1)} custom-call(bf16[3,128,768]{2,1,0:T(8,128)(2,1)S(1)} %choose.13.refs_6_.refs_0_, bf16[3,128,768]{2,1,0:T(8,128)(2,1)S(1)} %collective-permute-done.37.refs_1_, bf16[1024,6656]{1,0:T(8,128)(2,1)} %refs_2_.35, bf16[1024,6656]{1,0:T(8,128)(2,1)} %refs_3_.35, ...), custom_call_target="tpu_custom_call", output_to_operand_aliasing={{}: (5, {})} | custom-call | flops 1000 | bytes 1000 | tf_op jit(solution)/shard_map/backward_products/pallas_call | solution.py:49
  181.0 6.7 %collective-permute-done.44.refs_2_ = bf16[3,128,768]{2,1,0:T(8,128)(2,1)S(1)} collective-permute-done((bf16[3,128,768]{2,1,0:T(8,128)(2,1)S(1)}, bf16[3,128,768]{2,1,0:T(8,128)(2,1)S(1)}, u32[]{:S(2)}, u32[]{:S(2)}) %collective-permute-start.44) | collective-permute-done | bytes 589856 | tf_op jit(solution)/shard_map/ppermute | solution.py:266
  187.7 4.0 %backward_products.18.refs_7_.refs_5_ = f32[2,256,1024]{2,1,0:T(8,128)S(1)} custom-call(bf16[3,128,768]{2,1,0:T(8,128)(2,1)S(1)} %choose.14.refs_6_.refs_0_, bf16[3,128,768]{2,1,0:T(8,128)(2,1)S(1)} %collective-permute-done.43.refs_1_, bf16[1024,6656]{1,0:T(8,128)(2,1)} %refs_2_.35, bf16[1024,6656]{1,0:T(8,128)(2,1)} %refs_3_.35, ...), custom_call_target="tpu_custom_call", output_to_operand_aliasing={{}: (5, {})} | custom-call | flops 1000 | bytes 1000 | tf_op jit(solution)/shard_map/backward_products/pallas_call | solution.py:49
  201.9 6.2 %backward_products.21 = (f32[2,256,1024]{2,1,0:T(8,128)S(1)}, bf16[1024,6656]{1,0:T(8,128)(2,1)}, bf16[1024,6656]{1,0:T(8,128)(2,1)}, bf16[6656,1024]{1,0:T(8,128)(2,1)}) custom-call(bf16[3,128,768]{2,1,0:T(8,128)(2,1)S(1)} %choose.15.refs_6_.refs_0_, ...), custom_call_target="tpu_custom_call", output_to_operand_aliasing={{0}: (5, {}), {1}: (8, {}), {2}: (9, {}), {3}: (10, {})} | custom-call | flops 1000 | bytes 1000 | tf_op jit(solution)/shard_map/backward_products/pallas_call | solution.py:49
  208.1 6.2 %backward_products.22 = (f32[2,256,1024]{2,1,0:T(8,128)S(1)}, bf16[1024,6656]{1,0:T(8,128)(2,1)}, bf16[1024,6656]{1,0:T(8,128)(2,1)}, bf16[6656,1024]{1,0:T(8,128)(2,1)}) custom-call(bf16[3,128,768]{2,1,0:T(8,128)(2,1)S(1)} %choose.16.refs_11_.refs_0_, ...), custom_call_target="tpu_custom_call", output_to_operand_aliasing={{0}: (5, {}), {1}: (8, {}), {2}: (9, {}), {3}: (10, {})} | custom-call | flops 1000 | bytes 1000 | tf_op jit(solution)/shard_map/backward_products/pallas_call | solution.py:49
  228.8 6.7 %collective-permute-done.52 = bf16[2,64,1024]{2,1,0:T(8,128)(2,1)S(1)} collective-permute-done((bf16[2,64,1024]{2,1,0:T(8,128)(2,1)S(1)}, bf16[2,64,1024]{2,1,0:T(8,128)(2,1)S(1)}, u32[]{:S(2)}, u32[]{:S(2)}) %collective-permute-start.52) | collective-permute-done | bytes 262176 | tf_op jit(solution)/shard_map/ppermute | solution.py:321
  (196 shorter events, 112.0 us)
Async XLA Ops:
  30.5 17.9 %collective-permute-start.11 = (bf16[3,128,768]{2,1,0:T(8,128)(2,1)S(1)}, bf16[3,128,768]{2,1,0:T(8,128)(2,1)S(1)}, u32[]{:S(2)}, u32[]{:S(2)}) collective-permute-start(bf16[3,128,768]{2,1,0:T(8,128)(2,1)S(1)} %chip_sum.9.refs_2_.refs_0_), channel_id=1, source_target_pairs={{0,8},{4,12},{24,16},{28,20},{1,9},{5,13},{25,17},{29,21},{2,10},{... | collective-permute-start | bytes 1769480 | tf_op jit(solution)/shard_map/ppermute | solution.py:249
  46.8 17.5 %collective-permute-start.15 = (bf16[3,128,768]{2,1,0:T(8,128)(2,1)S(1)}, bf16[3,128,768]{2,1,0:T(8,128)(2,1)S(1)}, u32[]{:S(2)}, u32[]{:S(2)}) collective-permute-start(bf16[3,128,768]{2,1,0:T(8,128)(2,1)S(1)} %chip_sum.10.refs_5_.refs_0_), channel_id=1, source_target_pairs={{0,8},{4,12},{24,16},{28,20},{1,9},{5,13},{25,17},{29,21},{2,10},{... | collective-permute-start | bytes 1769480 | tf_op jit(solution)/shard_map/ppermute | solution.py:249
  58.3 23.2 %collective-permute-start.20 = (bf16[3,128,768]{2,1,0:T(8,128)(2,1)S(1)}, bf16[3,128,768]{2,1,0:T(8,128)(2,1)S(1)}, u32[]{:S(2)}, u32[]{:S(2)}) collective-permute-start(bf16[3,128,768]{2,1,0:T(8,128)(2,1)S(1)} %chip_sum.11.refs_2_.refs_0_), channel_id=1, source_target_pairs={{0,8},{4,12},{24,16},{28,20},{1,9},{5,13},{25,17},{29,21},{2,10},{... | collective-permute-start | bytes 1769480 | tf_op jit(solution)/shard_map/ppermute | solution.py:249
  64.4 19.6 %collective-permute-start.19 = (bf16[3,128,768]{2,1,0:T(8,128)(2,1)S(1)}, bf16[3,128,768]{2,1,0:T(8,128)(2,1)S(1)}, u32[]{:S(2)}, u32[]{:S(2)}) collective-permute-start(bf16[3,128,768]{2,1,0:T(8,128)(2,1)S(1)} %half_sum.10.refs_2_.refs_0_), channel_id=1, source_target_pairs={{8,16},{12,20},{16,8},{20,12},{9,17},{13,21},{17,9},{21,13},{10,18... | collective-permute-start | bytes 1769480 | tf_op jit(solution)/shard_map/ppermute | solution.py:257
  65.5 21.0 %collective-permute-start.18 = (bf16[3,128,768]{2,1,0:T(8,128)(2,1)S(1)}, bf16[3,128,768]{2,1,0:T(8,128)(2,1)}, u32[]{:S(2)}, u32[]{:S(2)}) collective-permute-start(bf16[3,128,768]{2,1,0:T(8,128)(2,1)S(1)} %activations.9.refs_2_.refs_0_), channel_id=1, source_target_pairs={{8,0},{12,4},{16,24},{20,28},{9,1},{13,5},{17,25},{21,29},{10,2},{... | collective-permute-start | bytes 1769480 | tf_op jit(solution)/shard_map/ppermute | solution.py:266
  72.0 16.8 %collective-permute-start.17 = (bf16[3,128,768]{2,1,0:T(8,128)(2,1)}, bf16[3,128,768]{2,1,0:T(8,128)(2,1)}, u32[]{:S(2)}, u32[]{:S(2)}) collective-permute-start(bf16[3,128,768]{2,1,0:T(8,128)(2,1)} %get-tuple-element.72), channel_id=1, source_target_pairs={{0,4},{4,0},{8,12},{12,8},{16,20},{20,16},{24,28},{28,24},{1,5},{5... | collective-permute-start | bytes 1769480 | tf_op jit(solution)/shard_map/ppermute | solution.py:243
  72.1 27.6 %collective-permute-start.26 = (bf16[3,128,768]{2,1,0:T(8,128)(2,1)S(1)}, bf16[3,128,768]{2,1,0:T(8,128)(2,1)}, u32[]{:S(2)}, u32[]{:S(2)}) collective-permute-start(bf16[3,128,768]{2,1,0:T(8,128)(2,1)S(1)} %chip_sum.12.refs_2_.refs_0_), channel_id=1, source_target_pairs={{0,8},{4,12},{24,16},{28,20},{1,9},{5,13},{25,17},{29,21},{2,10},{... | collective-permute-start | bytes 1769480 | tf_op jit(solution)/shard_map/ppermute | solution.py:249
  82.5 20.8 %collective-permute-start.25 = (bf16[3,128,768]{2,1,0:T(8,128)(2,1)}, bf16[3,128,768]{2,1,0:T(8,128)(2,1)}, u32[]{:S(2)}, u32[]{:S(2)}) collective-permute-start(bf16[3,128,768]{2,1,0:T(8,128)(2,1)} %half_sum.11.refs_2_.refs_0_), channel_id=1, source_target_pairs={{8,16},{12,20},{16,8},{20,12},{9,17},{13,21},{17,9},{21,13},{10,18... | collective-permute-start | bytes 1769480 | tf_op jit(solution)/shard_map/ppermute | solution.py:257
  86.4 19.8 %collective-permute-start.24 = (bf16[3,128,768]{2,1,0:T(8,128)(2,1)S(1)}, bf16[3,128,768]{2,1,0:T(8,128)(2,1)}, u32[]{:S(2)}, u32[]{:S(2)}) collective-permute-start(bf16[3,128,768]{2,1,0:T(8,128)(2,1)S(1)} %activations.10.refs_3_.refs_0_), channel_id=1, source_target_pairs={{8,0},{12,4},{16,24},{20,28},{9,1},{13,5},{17,25},{21,29},{10,2},{... | collective-permute-start | bytes 1769480 | tf_op jit(solution)/shard_map/ppermute | solution.py:266
  88.9 18.6 %collective-permute-start.23 = (bf16[3,128,768]{2,1,0:T(8,128)(2,1)S(1)}, bf16[3,128,768]{2,1,0:T(8,128)(2,1)S(1)}, u32[]{:S(2)}, u32[]{:S(2)}) collective-permute-start(bf16[3,128,768]{2,1,0:T(8,128)(2,1)S(1)} %choose.9.refs_2_.refs_0_), channel_id=1, source_target_pairs={{0,4},{4,0},{8,12},{12,8},{16,20},{20,16},{24,28},{28,24},{1,5},{5... | collective-permute-start | bytes 1769480 | tf_op jit(solution)/shard_map/ppermute | solution.py:277
  91.5 32.7 %collective-permute-start.22 = (bf16[3,128,768]{2,1,0:T(8,128)(2,1)}, bf16[3,128,768]{2,1,0:T(8,128)(2,1)}, u32[]{:S(2)}, u32[]{:S(2)}) collective-permute-start(bf16[3,128,768]{2,1,0:T(8,128)(2,1)} %copy-done.6), channel_id=1, source_target_pairs={{0,8},{4,12},{24,16},{28,20},{1,9},{5,13},{25,17},{29,21},{2,10},{... | collective-permute-start | bytes 1769480 | tf_op jit(solution)/shard_map/ppermute | solution.py:249
  101.8 24.3 %collective-permute-start.31 = (bf16[3,128,768]{2,1,0:T(8,128)(2,1)}, bf16[3,128,768]{2,1,0:T(8,128)(2,1)}, u32[]{:S(2)}, u32[]{:S(2)}) collective-permute-start(bf16[3,128,768]{2,1,0:T(8,128)(2,1)} %half_sum.12.refs_2_.refs_0_), channel_id=1, source_target_pairs={{8,16},{12,20},{16,8},{20,12},{9,17},{13,21},{17,9},{21,13},{10,18... | collective-permute-start | bytes 1769480 | tf_op jit(solution)/shard_map/ppermute | solution.py:257
  104.9 24.2 %collective-permute-start.30 = (bf16[3,128,768]{2,1,0:T(8,128)(2,1)S(1)}, bf16[3,128,768]{2,1,0:T(8,128)(2,1)}, u32[]{:S(2)}, u32[]{:S(2)}) collective-permute-start(bf16[3,128,768]{2,1,0:T(8,128)(2,1)S(1)} %activations.11.refs_3_.refs_0_), channel_id=1, source_target_pairs={{8,0},{12,4},{16,24},{20,28},{9,1},{13,5},{17,25},{21,29},{10,2},{... | collective-permute-start | bytes 1769480 | tf_op jit(solution)/shard_map/ppermute | solution.py:266
  107.3 23.1 %collective-permute-start.29 = (bf16[3,128,768]{2,1,0:T(8,128)(2,1)S(1)}, bf16[3,128,768]{2,1,0:T(8,128)(2,1)S(1)}, u32[]{:S(2)}, u32[]{:S(2)}) collective-permute-start(bf16[3,128,768]{2,1,0:T(8,128)(2,1)S(1)} %choose.10.refs_7_.refs_0_), channel_id=1, source_target_pairs={{0,4},{4,0},{8,12},{12,8},{16,20},{20,16},{24,28},{28,24},{1,5},{5... | collective-permute-start | bytes 1769480 | tf_op jit(solution)/shard_map/ppermute | solution.py:277
  108.3 32.9 %collective-permute-start.28 = (bf16[3,128,768]{2,1,0:T(8,128)(2,1)}, bf16[3,128,768]{2,1,0:T(8,128)(2,1)}, u32[]{:S(2)}, u32[]{:S(2)}) collective-permute-start(bf16[3,128,768]{2,1,0:T(8,128)(2,1)} %copy-done), channel_id=1, source_target_pairs={{0,8},{4,12},{24,16},{28,20},{1,9},{5,13},{25,17},{29,21},{2,10},{... | collective-permute-start | bytes 1769480 | tf_op jit(solution)/shard_map/ppermute | solution.py:249
  125.5 17.6 %collective-permute-start.27 = (bf16[3,128,768]{2,1,0:T(8,128)(2,1)S(1)}, bf16[3,128,768]{2,1,0:T(8,128)(2,1)S(1)}, u32[]{:S(2)}, u32[]{:S(2)}) collective-permute-start(bf16[3,128,768]{2,1,0:T(8,128)(2,1)S(1)} %half_sum.13.refs_2_.refs_0_), channel_id=1, source_target_pairs={{8,16},{12,20},{16,8},{20,12},{9,17},{13,21},{17,9},{21,13},{10,18... | collective-permute-start | bytes 1769480 | tf_op jit(solution)/shard_map/ppermute | solution.py:257
  127.7 17.3 %collective-permute-start.36 = (bf16[3,128,768]{2,1,0:T(8,128)(2,1)S(1)}, bf16[3,128,768]{2,1,0:T(8,128)(2,1)S(1)}, u32[]{:S(2)}, u32[]{:S(2)}) collective-permute-start(bf16[3,128,768]{2,1,0:T(8,128)(2,1)S(1)} %activations.12.refs_3_.refs_0_), channel_id=1, source_target_pairs={{8,0},{12,4},{16,24},{20,28},{9,1},{13,5},{17,25},{21,29},{10,2},{... | collective-permute-start | bytes 1769480 | tf_op jit(solution)/shard_map/ppermute | solution.py:266
  130.4 25.3 %collective-permute-start.34 = (bf16[3,128,768]{2,1,0:T(8,128)(2,1)S(1)}, bf16[3,128,768]{2,1,0:T(8,128)(2,1)S(1)}, u32[]{:S(2)}, u32[]{:S(2)}) collective-permute-start(bf16[3,128,768]{2,1,0:T(8,128)(2,1)S(1)} %copy-done.5), channel_id=1, source_target_pairs={{0,8},{4,12},{24,16},{28,20},{1,9},{5,13},{25,17},{29,21},{2,10},{... | collective-permute-start | bytes 1769480 | tf_op jit(solution)/shard_map/ppermute | solution.py:249
  143.4 17.3 %collective-permute-start.32 = (bf16[3,128,768]{2,1,0:T(8,128)(2,1)S(1)}, bf16[3,128,768]{2,1,0:T(8,128)(2,1)S(1)}, u32[]{:S(2)}, u32[]{:S(2)}) collective-permute-start(bf16[3,128,768]{2,1,0:T(8,128)(2,1)S(1)} %activations.13.refs_3_.refs_0_), channel_id=1, source_target_pairs={{8,0},{12,4},{16,24},{20,28},{9,1},{13,5},{17,25},{21,29},{10,2},{... | collective-permute-start | bytes 1769480 | tf_op jit(solution)/shard_map/ppermute | solution.py:266
  145.2 19.7 %collective-permute-start.41 = (bf16[3,128,768]{2,1,0:T(8,128)(2,1)S(1)}, bf16[3,128,768]{2,1,0:T(8,128)(2,1)S(1)}, u32[]{:S(2)}, u32[]{:S(2)}) collective-permute-start(bf16[3,128,768]{2,1,0:T(8,128)(2,1)S(1)} %chip_sum.16.refs_2_.refs_0_), channel_id=1, source_target_pairs={{0,8},{4,12},{24,16},{28,20},{1,9},{5,13},{25,17},{29,21},{2,10},{... | collective-permute-start | bytes 1769480 | tf_op jit(solution)/shard_map/ppermute | solution.py:249
  156.9 17.3 %collective-permute-start.39 = (bf16[3,128,768]{2,1,0:T(8,128)(2,1)S(1)}, bf16[3,128,768]{2,1,0:T(8,128)(2,1)S(1)}, u32[]{:S(2)}, u32[]{:S(2)}) collective-permute-start(bf16[3,128,768]{2,1,0:T(8,128)(2,1)S(1)} %activations.14.refs_3_.refs_0_), channel_id=1, source_target_pairs={{8,0},{12,4},{16,24},{20,28},{9,1},{13,5},{17,25},{21,29},{10,2},{... | collective-permute-start | bytes 1769480 | tf_op jit(solution)/shard_map/ppermute | solution.py:266
  170.2 17.4 %collective-permute-start.44 = (bf16[3,128,768]{2,1,0:T(8,128)(2,1)S(1)}, bf16[3,128,768]{2,1,0:T(8,128)(2,1)S(1)}, u32[]{:S(2)}, u32[]{:S(2)}) collective-permute-start(bf16[3,128,768]{2,1,0:T(8,128)(2,1)S(1)} %activations.15.refs_3_.refs_0_), channel_id=1, source_target_pairs={{8,0},{12,4},{16,24},{20,28},{9,1},{13,5},{17,25},{21,29},{10,2},{... | collective-permute-start | bytes 1769480 | tf_op jit(solution)/shard_map/ppermute | solution.py:266
  179.0 21.3 %collective-permute-start.47 = (bf16[3,128,768]{2,1,0:T(8,128)(2,1)S(1)}, bf16[3,128,768]{2,1,0:T(8,128)(2,1)S(1)}, u32[]{:S(2)}, u32[]{:S(2)}) collective-permute-start(bf16[3,128,768]{2,1,0:T(8,128)(2,1)S(1)} %activations.16.refs_3_.refs_0_), channel_id=1, source_target_pairs={{8,0},{12,4},{16,24},{20,28},{9,1},{13,5},{17,25},{21,29},{10,2},{... | collective-permute-start | bytes 1769480 | tf_op jit(solution)/shard_map/ppermute | solution.py:266
  180.3 18.0 %collective-permute-start.42 = (bf16[3,128,512]{2,1,0:T(8,128)(2,1)S(1)}, bf16[3,128,512]{2,1,0:T(8,128)(2,1)S(1)}, u32[]{:S(2)}, u32[]{:S(2)}) collective-permute-start(bf16[3,128,512]{2,1,0:T(8,128)(2,1)S(1)} %half_sum.17.refs_2_.refs_0_), channel_id=1, source_target_pairs={{8,16},{12,20},{16,8},{20,12},{9,17},{13,21},{17,9},{21,13},{10,18... | collective-permute-start | bytes 1179656 | tf_op jit(solution)/shard_map/ppermute | solution.py:257
  (48 other events, 405.8 us)

commit v2 on v1

--- a/solution.py
+++ b/solution.py
@@ -10,7 +10,7 @@
 F32 = jnp.float32
 BF16 = jnp.bfloat16
 MOST_CHUNKS = 9
-KERNEL_VMEM = 42 * 1024 * 1024
+KERNEL_VMEM = 24 * 1024 * 1024
 ANYWHERE = pl.BlockSpec(memory_space=pl.ANY)
 
 
@@ -42,6 +42,7 @@
 
     def call(self, kernel, grid, in_specs, out_specs, out_shape, aliases, vmem, cost, name, *args):
         extra = [] if self.last is None or any(self.last is a for a in args) else [self.last]
+        extra = [pltpu.with_memory_space_constraint(e, pltpu.HBM) if e.ndim == 2 else e for e in extra]
 
         def body(*refs):
             kernel(*refs[: len(args)], *refs[len(args) + len(extra) :])
@@ -61,38 +62,58 @@
         return out
 
 
-def forward_kernel(x_ref, c_ref, gate_ref, up_ref, down_ref, mine_ref, theirs_ref):
+def split_store(values, mine_ref, theirs_ref):
     half = mine_ref.shape[1]
-    sums = (
-        jnp.dot(x_ref[...], gate_ref[...], preferred_element_type=F32),
-        jnp.dot(x_ref[...], up_ref[...], preferred_element_type=F32),
-        contract_last(c_ref[...], down_ref[...]),
-    )
-    for index, value in enumerate(sums):
+    for index, value in enumerate(values):
         mine_ref[index] = value[:half].astype(BF16)
         theirs_ref[index] = value[half:].astype(BF16)
 
 
-def forward(order, x, c, gate, up, down, start, width):
-    tokens, depth = x.shape
+def gate_up_sums(x_ref, gate_ref, up_ref):
+    return [
+        jnp.dot(x_ref[...], w_ref[...], preferred_element_type=F32) for w_ref in (gate_ref, up_ref)
+    ]
+
+
+def forward_kernel(x_ref, gate_ref, up_ref, c_ref, down_ref, mine_ref, theirs_ref):
+    sums = gate_up_sums(x_ref, gate_ref, up_ref)
+    split_store(sums + [contract_last(c_ref[...], down_ref[...])], mine_ref, theirs_ref)
+
+
+def gate_up_kernel(x_ref, gate_ref, up_ref, mine_ref, theirs_ref):
+    split_store(gate_up_sums(x_ref, gate_ref, up_ref), mine_ref, theirs_ref)
+
+
+def back_kernel(c_ref, down_ref, mine_in_ref, theirs_in_ref, mine_ref, theirs_ref):
+    split_store([contract_last(c_ref[...], down_ref[...])], mine_ref, theirs_ref)
+
+
+def forward(order, x, c, weights, start, width, partly=None):
+    tokens, depth = (c if x is None else x).shape
     tile = tile_of(width)
     first = start // tile
     half = tokens // 2
+    gate, up, down = weights
     part = jax.ShapeDtypeStruct((3, half, width), BF16)
     column = pl.BlockSpec((depth, tile), lambda i: (0, first + i))
     row = pl.BlockSpec((tile, depth), lambda i: (first + i, 0))
-    piece = pl.BlockSpec((3, half, tile), lambda i: (0, 0, i))
+    block = whole((tokens, depth))
+    if c is None:
+        kernel, specs, args = gate_up_kernel, [block, column, column], [x, gate, up]
+        piece = pl.BlockSpec((2, half, tile), lambda i: (0, 0, i))
+        aliases = {}
+    elif x is None:
+        kernel, specs, args = back_kernel, [block, row, ANYWHERE, ANYWHERE], [c, down, *partly]
+        piece = pl.BlockSpec((1, half, tile), lambda i: (2, 0, i))
+        aliases = {2: 0, 3: 1}
+    else:
+        kernel, specs = forward_kernel, [block, column, column, block, row]
+        args = [x, gate, up, c, down]
+        piece = pl.BlockSpec((3, half, tile), lambda i: (0, 0, i))
+        aliases = {}
     return order.call(
-        forward_kernel,
-        (width // tile,),
-        [whole(x.shape), whole(c.shape), column, column, row],
-        [piece, piece],
-        [part, part],
-        {},
-        KERNEL_VMEM,
-        1000,
-        "forward_sums",
-        x, c, gate, up, down,
+        kernel, (width // tile,), specs, [piece, piece], [part, part], aliases, KERNEL_VMEM, 1000,
+        "forward_sums", *args,
     )
 
 
@@ -102,6 +123,41 @@
     shape = jax.ShapeDtypeStruct(args[0].shape, BF16)
     return order.call(
         kernel, (1,), specs, [piece], [shape], {}, KERNEL_VMEM, 1000, name, *args
+    )[0]
+
+
+def assemble_kernel(flag_ref, *refs):
+    blocks, out_ref = refs[:-1], refs[-1]
+    count, rows = len(blocks), blocks[0].shape[0]
+    for core in range(2):
+
+        @pl.when(flag_ref[0] == core)
+        def _():
+            for index, block in enumerate(blocks):
+                place = (index + core * (count // 2)) % count
+                out_ref[pl.ds(place * rows, rows), :] = block[...]
+
+
+def assemble(order, flag, blocks):
+    rows, depth = blocks[0].shape
+    shape = (rows * len(blocks), depth)
+    return order.call(
+        assemble_kernel, (1,),
+        [pl.BlockSpec(memory_space=pltpu.SMEM)] + [whole((rows, depth))] * len(blocks),
+        [whole(shape)], [jax.ShapeDtypeStruct(shape, BF16)], {}, KERNEL_VMEM, 1000,
+        "assemble_tokens", flag, *blocks,
+    )[0]
+
+
+def transpose_kernel(x_ref, xt_ref):
+    xt_ref[...] = x_ref[...].T
+
+
+def transpose(order, x):
+    shape = x.shape[::-1]
+    return order.call(
+        transpose_kernel, (1,), [whole(x.shape)], [whole(shape)],
+        [jax.ShapeDtypeStruct(shape, BF16)], {}, KERNEL_VMEM, 1000, "transpose_tokens", x,
     )[0]
 
 
@@ -182,7 +238,7 @@
             specs += [ANYWHERE]
             args += [grad]
         out_specs += [column, column, row]
-        shapes += [jax.ShapeDtypeStruct(w.shape, BF16) for w in weights]
+        shapes += [pltpu.HBM(w.shape, BF16) for w in weights]
 
     def kernel(*refs):
         ins, outs = refs[: len(args)], refs[len(args) :]
@@ -215,31 +271,31 @@
         jnp.where((chip == j) | (chip == chips - 1 - j), 1, 0).astype(jnp.int32).reshape(1)
         for j in range(middle - 1)
     ]
-    weights = [gate_weight, up_weight, down_weight]
-
-    def gather(block):
-        blocks = [block] + [
+    weights = [
+        pltpu.with_memory_space_constraint(w, pltpu.HBM)
+        for w in (gate_weight, up_weight, down_weight)
+    ]
+
+    order = Order()
+    core_flag = core.astype(jnp.int32).reshape(1)
+
+    def travel(block):
+        return [block] + [
             lax.ppermute(block, "col", [(s, s ^ j) for s in range(n_col)]) for j in range(1, n_col)
         ]
-        low = jnp.concatenate(blocks[: n_col // 2], axis=0)
-        high = jnp.concatenate(blocks[n_col // 2 :], axis=0)
-        return jnp.concatenate(
-            [jnp.where(core == 0, low, high), jnp.where(core == 0, high, low)], axis=0
-        )
-
-    x = gather(tokens)
-    c = gather(cotangent)
-    xt = x.T
-
-    order = Order()
+
+    token_blocks, cotangent_blocks = travel(tokens), travel(cotangent)
+    x = assemble(order, core_flag, token_blocks)
+
     chunks = chunks_of(gate_weight.shape[1])
     count = len(chunks)
     swapped, partial, arrived, acts, other = {}, {}, {}, {}, {}
     state = [None, None]
 
-    def step_sums(k):
-        if 0 <= k < count:
-            mine, theirs = forward(order, x, c, *weights, *chunks[k])
+    def step_sums(k, partly=None):
+        if 0 <= k < count:
+            left = x if partly is None else None
+            mine, theirs = forward(order, left, c, weights, *chunks[k], partly)
             swapped[k] = (mine, lax.ppermute(theirs, "row", siblings))
 
     def step_chip(k):
@@ -282,8 +338,10 @@
                 order, acts[k], other[k], xt, c, weights, chunks[k][0], *state, parts
             )
 
-    step_sums(0)
-    step_sums(1)
+    early = [forward(order, x, None, weights, *chunks[k]) for k in range(2)]
+    c = assemble(order, core_flag, cotangent_blocks)
+    step_sums(0, early[0])
+    step_sums(1, early[1])
     step_chip(0)
     step_chip(1)
     summed = 2
@@ -293,6 +351,8 @@
         summed = fresh.stop
         for j in fresh:
             step_sums(j)
+        if k == 0:
+            xt = transpose(order, x)
         step_half(k)
         step_act(k - 1)
         step_choose(k - 2)

time: 239 us -> 228 us (0.954)
  starting transfers between devices: 79.8 us -> 73.7 us
  local copies, waits for them, and re-layouts: 11 us -> 6.57 us
  Pallas kernels: 112 us -> 116 us
  waiting for transfers between devices: 30 us -> 27.2 us
    ppermute x9, starting transfers between devices: 42.2 us -> 36.3 us  [step_chip(): arrived[k] = lax.ppermute(partial[k], 'row', inward[0])]
    ppermute x6, waiting for transfers between devices: 6.03 us -> 2.01 us  [travel(): lax.ppermute(block, 'col', [(s, s ^ j) for s in range(n_col)])]
    pallas_call x58 -> x63, Pallas kernels: 112 us -> 116 us  [call(): pl.pallas_call(body, grid=grid, in_specs=list(in_specs) + [ANYWHERE] * le...]
    unnamed x40 -> x32, local copies, waits for them, and re-layouts: 8.8 us -> 5.71 us
  transfers between devices with their start and end apart: 54 -> 54, of which waited for: 12 -> 11; matrix products, arithmetic and copies ran while one was open for 1% -> 0% of each run, Pallas kernels for 45% -> 49%
where the time goes in v2:
time: 228 us; the launch traced here: 226 us
  Pallas kernels  116 us (51%)
  starting transfers between devices  73.7 us (32%)
  waiting for transfers between devices  27.2 us (12%)
  local copies, waits for them, and re-layouts  6.57 us (3%)
    pallas_call x63, Pallas kernels, call(): pl.pallas_call(body, grid=grid, in_specs=list(in_specs) + [ANYWHERE] * le...  116 us
    ppermute x9, starting transfers between devices, step_chip(): arrived[k] = lax.ppermute(partial[k], 'row', inward[0])  36.3 us
    ppermute x9, waiting for transfers between devices, step_act(): arrived[k] = lax.ppermute(acts[k], 'row', back)  16.4 us
    ppermute x9, starting transfers between devices, step_act(): arrived[k] = lax.ppermute(acts[k], 'row', back)  11.8 us
    ppermute x6, starting transfers between devices, travel(): lax.ppermute(block, 'col', [(s, s ^ j) for s in range(n_col)])  10.5 us
    ppermute x9, starting transfers between devices, step_half(): arrived[k] = lax.ppermute(partial[k], 'row', across)  7.19 us
    ppermute x3, waiting for transfers between devices, shards(): lax.ppermute(piece, 'col', [(s, s ^ j) for s in range(n_col)]).astype(F32)  5.79 us
    unnamed x32, local copies, waits for them, and re-layouts  5.71 us
  transfers between devices with their start and end apart: 54, of which 11 were waited for; matrix products, arithmetic and copies ran while one was open for 0% of the time, Pallas kernels for 49%

profile of v2, /device:TPU:0, one launch (start us, length us, event | category | flops | bytes accessed | tf_op | source)
XLA Modules:
  0.0 226.2 jit_solution(16048116506587646162)
XLA Ops:
  14.1 3.3 %forward_sums.11 = (bf16[3,128,768]{2,1,0:T(8,128)(2,1)S(1)}, bf16[3,128,768]{2,1,0:T(8,128)(2,1)S(1)}) custom-call(bf16[256,1024]{1,0:T(8,128)(2,1)S(1)} %assemble_tokens.2.refs_0_, bf16[1024,6656]{1,0:T(8,128)(2,1)} %refs_2_.35, bf16[1024,6656]{1,0:T(8,128)(2,1)} %refs_3_.17), custom_call_target="tpu_custom_call" | custom-call | flops 1000 | bytes 1000 | tf_op jit(solution)/shard_map/forward_sums/pallas_call | solution.py:50
  17.5 3.4 %forward_sums.12 = (bf16[3,128,768]{2,1,0:T(8,128)(2,1)S(1)}, bf16[3,128,768]{2,1,0:T(8,128)(2,1)S(1)}) custom-call(bf16[256,1024]{1,0:T(8,128)(2,1)S(1)} %assemble_tokens.2.refs_0_, bf16[1024,6656]{1,0:T(8,128)(2,1)} %refs_2_.35, bf16[1024,6656]{1,0:T(8,128)(2,1)} %refs_3_.17, bf16[3,128,768]{2,1,0:T(8,128)(2,1)S(1)} %get-tuple-element.59.refs_3_.refs_2_), custom_call_target="tpu_custom_call" | custom-call | flops 1000 | bytes 1000 | tf_op jit(solution)/shard_map/forward_sums/pallas_call | solution.py:50
  32.1 4.0 %forward_sums.15 = (bf16[3,128,768]{2,1,0:T(8,128)(2,1)S(1)}, bf16[3,128,768]{2,1,0:T(8,128)(2,1)S(1)}) custom-call(bf16[256,1024]{1,0:T(8,128)(2,1)S(1)} %assemble_tokens.2.refs_0_, bf16[1024,6656]{1,0:T(8,128)(2,1)} %refs_2_.35, bf16[1024,6656]{1,0:T(8,128)(2,1)} %refs_3_.17, bf16[256,1024]{1,0:T(8,128)(2,1)S(1)} %assemble_tokens.3.refs_0_.refs_3_.refs_6_.refs_7_, ...), custom_call_target="tpu_custom_call" | custom-call | flops 1000 | bytes 1000 | tf_op jit(solution)/shard_map/forward_sums/pallas_call | solution.py:50
  36.3 4.0 %forward_sums.16 = (bf16[3,128,768]{2,1,0:T(8,128)(2,1)S(1)}, bf16[3,128,768]{2,1,0:T(8,128)(2,1)S(1)}) custom-call(bf16[256,1024]{1,0:T(8,128)(2,1)S(1)} %assemble_tokens.2.refs_0_, bf16[1024,6656]{1,0:T(8,128)(2,1)} %refs_2_.35, bf16[1024,6656]{1,0:T(8,128)(2,1)} %refs_3_.17, bf16[256,1024]{1,0:T(8,128)(2,1)S(1)} %assemble_tokens.3.refs_0_.refs_3_.refs_6_.refs_7_, ...), custom_call_target="tpu_custom_call" | custom-call | flops 1000 | bytes 1000 | tf_op jit(solution)/shard_map/forward_sums/pallas_call | solution.py:50
  40.8 4.0 %forward_sums.17 = (bf16[3,128,768]{2,1,0:T(8,128)(2,1)S(1)}, bf16[3,128,768]{2,1,0:T(8,128)(2,1)S(1)}) custom-call(bf16[256,1024]{1,0:T(8,128)(2,1)S(1)} %assemble_tokens.2.refs_0_, bf16[1024,6656]{1,0:T(8,128)(2,1)} %refs_2_.35, bf16[1024,6656]{1,0:T(8,128)(2,1)} %refs_3_.17, bf16[256,1024]{1,0:T(8,128)(2,1)S(1)} %assemble_tokens.3.refs_0_.refs_3_.refs_6_.refs_7_, ...), custom_call_target="tpu_custom_call" | custom-call | flops 1000 | bytes 1000 | tf_op jit(solution)/shard_map/forward_sums/pallas_call | solution.py:50
  50.4 4.0 %forward_sums.18 = (bf16[3,128,768]{2,1,0:T(8,128)(2,1)S(1)}, bf16[3,128,768]{2,1,0:T(8,128)(2,1)S(1)}) custom-call(bf16[256,1024]{1,0:T(8,128)(2,1)S(1)} %assemble_tokens.2.refs_0_, bf16[1024,6656]{1,0:T(8,128)(2,1)} %refs_2_.35, bf16[1024,6656]{1,0:T(8,128)(2,1)} %refs_3_.17, bf16[256,1024]{1,0:T(8,128)(2,1)S(1)} %assemble_tokens.3.refs_0_.refs_3_.refs_6_.refs_7_, ...), custom_call_target="tpu_custom_call" | custom-call | flops 1000 | bytes 1000 | tf_op jit(solution)/shard_map/forward_sums/pallas_call | solution.py:50
  54.7 4.0 %forward_sums.19 = (bf16[3,128,768]{2,1,0:T(8,128)(2,1)S(1)}, bf16[3,128,768]{2,1,0:T(8,128)(2,1)S(1)}) custom-call(bf16[256,1024]{1,0:T(8,128)(2,1)S(1)} %assemble_tokens.2.refs_0_, bf16[1024,6656]{1,0:T(8,128)(2,1)} %refs_2_.35, bf16[1024,6656]{1,0:T(8,128)(2,1)} %refs_3_.17, bf16[256,1024]{1,0:T(8,128)(2,1)S(1)} %assemble_tokens.3.refs_0_.refs_3_.refs_6_.refs_7_, ...), custom_call_target="tpu_custom_call" | custom-call | flops 1000 | bytes 1000 | tf_op jit(solution)/shard_map/forward_sums/pallas_call | solution.py:50
  59.1 4.9 %collective-permute-start.20 = (bf16[3,128,768]{2,1,0:T(8,128)(2,1)S(1)}, bf16[3,128,768]{2,1,0:T(8,128)(2,1)S(1)}, u32[]{:S(2)}, u32[]{:S(2)}) collective-permute-start(bf16[3,128,768]{2,1,0:T(8,128)(2,1)S(1)} %chip_sum.11.refs_2_.refs_0_), channel_id=1, source_target_pairs={{0,8},{4,12},{24,16},{28,20},{1,9},{5,13},{25,17},{29,21},{2,10},{... | collective-permute-start | bytes 1769480 | tf_op jit(solution)/shard_map/ppermute | solution.py:305
  67.6 4.9 %forward_sums.20 = (bf16[3,128,768]{2,1,0:T(8,128)(2,1)S(1)}, bf16[3,128,768]{2,1,0:T(8,128)(2,1)}) custom-call(bf16[256,1024]{1,0:T(8,128)(2,1)S(1)} %assemble_tokens.2.refs_0_, bf16[1024,6656]{1,0:T(8,128)(2,1)} %refs_2_.35, bf16[1024,6656]{1,0:T(8,128)(2,1)} %refs_3_.17, bf16[256,1024]{1,0:T(8,128)(2,1)S(1)} %assemble_tokens.3.refs_0_.refs_3_.refs_6_.refs_7_, ...), custom_call_target="tpu_custom_call" | custom-call | flops 1000 | bytes 1000 | tf_op jit(solution)/shard_map/forward_sums/pallas_call | solution.py:50
  72.6 6.2 %collective-permute-start.26 = (bf16[3,128,768]{2,1,0:T(8,128)(2,1)}, bf16[3,128,768]{2,1,0:T(8,128)(2,1)}, u32[]{:S(2)}, u32[]{:S(2)}) collective-permute-start(bf16[3,128,768]{2,1,0:T(8,128)(2,1)} %chip_sum.12.refs_2_.refs_0_), channel_id=1, source_target_pairs={{0,8},{4,12},{24,16},{28,20},{1,9},{5,13},{25,17},{29,21},{2,10},{... | collective-permute-start | bytes 1769480 | tf_op jit(solution)/shard_map/ppermute | solution.py:305
  91.4 5.1 %collective-permute-start.22 = (bf16[3,128,768]{2,1,0:T(8,128)(2,1)}, bf16[3,128,768]{2,1,0:T(8,128)(2,1)S(1)}, u32[]{:S(2)}, u32[]{:S(2)}) collective-permute-start(bf16[3,128,768]{2,1,0:T(8,128)(2,1)} %chip_sum.13.refs_5_.refs_0_), channel_id=1, source_target_pairs={{0,8},{4,12},{24,16},{28,20},{1,9},{5,13},{25,17},{29,21},{2,10},{... | collective-permute-start | bytes 1769480 | tf_op jit(solution)/shard_map/ppermute | solution.py:305
  106.1 3.4 %collective-permute-start.28 = (bf16[3,128,768]{2,1,0:T(8,128)(2,1)}, bf16[3,128,768]{2,1,0:T(8,128)(2,1)S(1)}, u32[]{:S(2)}, u32[]{:S(2)}) collective-permute-start(bf16[3,128,768]{2,1,0:T(8,128)(2,1)} %chip_sum.14.refs_2_.refs_0_), channel_id=1, source_target_pairs={{0,8},{4,12},{24,16},{28,20},{1,9},{5,13},{25,17},{29,21},{2,10},{... | collective-permute-start | bytes 1769480 | tf_op jit(solution)/shard_map/ppermute | solution.py:305
  109.5 6.4 %backward_products.13 = (f32[2,256,1024]{2,1,0:T(8,128)S(1)}, bf16[1024,6656]{1,0:T(8,128)(2,1)}, bf16[1024,6656]{1,0:T(8,128)(2,1)}, bf16[6656,1024]{1,0:T(8,128)(2,1)}) custom-call(bf16[3,128,768]{2,1,0:T(8,128)(2,1)S(1)} %choose.9.refs_2_.refs_0_, bf16[3,128,768]{2,1,0:T(8,128)(2,1)S(1)} %collective-permute-done.23.refs_1_, bf16[1024,6656]{1,0:T(8,128)(2,1)} %refs_2_.35, ...), custom_call_target="tpu_custom_call" | custom-call | flops 1000 | bytes 1000 | tf_op jit(solution)/shard_map/backward_products/pallas_call | solution.py:50
  119.7 4.6 %collective-permute-start.34 = (bf16[3,128,768]{2,1,0:T(8,128)(2,1)S(1)}, bf16[3,128,768]{2,1,0:T(8,128)(2,1)S(1)}, u32[]{:S(2)}, u32[]{:S(2)}) collective-permute-start(bf16[3,128,768]{2,1,0:T(8,128)(2,1)S(1)} %copy-done.7), channel_id=1, source_target_pairs={{0,8},{4,12},{24,16},{28,20},{1,9},{5,13},{25,17},{29,21},{2,10},{... | collective-permute-start | bytes 1769480 | tf_op jit(solution)/shard_map/ppermute | solution.py:305
  124.3 6.2 %backward_products.14 = (f32[2,256,1024]{2,1,0:T(8,128)S(1)}, bf16[1024,6656]{1,0:T(8,128)(2,1)}, bf16[1024,6656]{1,0:T(8,128)(2,1)}, bf16[6656,1024]{1,0:T(8,128)(2,1)}) custom-call(bf16[3,128,768]{2,1,0:T(8,128)(2,1)S(1)} %choose.10.refs_7_.refs_0_, ...), custom_call_target="tpu_custom_call", output_to_operand_aliasing={{0}: (5, {}), {1}: (8, {}), {2}: (9, {}), {3}: (10, {})} | custom-call | flops 1000 | bytes 1000 | tf_op jit(solution)/shard_map/backward_products/pallas_call | solution.py:50
  138.8 6.2 %backward_products.15 = (f32[2,256,1024]{2,1,0:T(8,128)S(1)}, bf16[1024,6656]{1,0:T(8,128)(2,1)}, bf16[1024,6656]{1,0:T(8,128)(2,1)}, bf16[6656,1024]{1,0:T(8,128)(2,1)}) custom-call(bf16[3,128,768]{2,1,0:T(8,128)(2,1)S(1)} %choose.11.refs_11_.refs_0_, ...), custom_call_target="tpu_custom_call", output_to_operand_aliasing={{0}: (5, {}), {1}: (8, {}), {2}: (9, {}), {3}: (10, {})} | custom-call | flops 1000 | bytes 1000 | tf_op jit(solution)/shard_map/backward_products/pallas_call | solution.py:50
  150.2 4.0 %backward_products.16.refs_2_.refs_5_ = f32[2,256,1024]{2,1,0:T(8,128)S(1)} custom-call(bf16[3,128,768]{2,1,0:T(8,128)(2,1)S(1)} %choose.12.refs_11_.refs_0_, bf16[3,128,768]{2,1,0:T(8,128)(2,1)S(1)} %collective-permute-done.38.refs_1_, bf16[1024,6656]{1,0:T(8,128)(2,1)} %refs_2_.35, bf16[1024,6656]{1,0:T(8,128)(2,1)} %refs_3_.17, ...), custom_call_target="tpu_custom_call", output_to_operand_aliasing={{}: (5, {})} | custom-call | flops 1000 | bytes 1000 | tf_op jit(solution)/shard_map/backward_products/pallas_call | solution.py:50
  155.1 4.1 %collective-permute-start.21 = (bf16[3,128,512]{2,1,0:T(8,128)(2,1)S(1)}, bf16[3,128,512]{2,1,0:T(8,128)(2,1)S(1)}, u32[]{:S(2)}, u32[]{:S(2)}) collective-permute-start(bf16[3,128,512]{2,1,0:T(8,128)(2,1)S(1)} %chip_sum.17.refs_2_.refs_0_), channel_id=1, source_target_pairs={{0,8},{4,12},{24,16},{28,20},{1,9},{5,13},{25,17},{29,21},{2,10},{... | collective-permute-start | bytes 1179656 | tf_op jit(solution)/shard_map/ppermute | solution.py:305
  163.7 4.1 %backward_products.17.refs_2_.refs_5_ = f32[2,256,1024]{2,1,0:T(8,128)S(1)} custom-call(bf16[3,128,768]{2,1,0:T(8,128)(2,1)S(1)} %choose.13.refs_6_.refs_0_, bf16[3,128,768]{2,1,0:T(8,128)(2,1)S(1)} %collective-permute-done.37.refs_1_, bf16[1024,6656]{1,0:T(8,128)(2,1)} %refs_2_.35, bf16[1024,6656]{1,0:T(8,128)(2,1)} %refs_3_.17, ...), custom_call_target="tpu_custom_call", output_to_operand_aliasing={{}: (5, {})} | custom-call | flops 1000 | bytes 1000 | tf_op jit(solution)/shard_map/backward_products/pallas_call | solution.py:50
  170.3 6.7 %collective-permute-done.44.refs_2_ = bf16[3,128,768]{2,1,0:T(8,128)(2,1)S(1)} collective-permute-done((bf16[3,128,768]{2,1,0:T(8,128)(2,1)S(1)}, bf16[3,128,768]{2,1,0:T(8,128)(2,1)S(1)}, u32[]{:S(2)}, u32[]{:S(2)}) %collective-permute-start.44) | collective-permute-done | bytes 589856 | tf_op jit(solution)/shard_map/ppermute | solution.py:322
  177.1 4.2 %backward_products.18.refs_7_.refs_5_ = f32[2,256,1024]{2,1,0:T(8,128)S(1)} custom-call(bf16[3,128,768]{2,1,0:T(8,128)(2,1)S(1)} %choose.14.refs_6_.refs_0_, bf16[3,128,768]{2,1,0:T(8,128)(2,1)S(1)} %collective-permute-done.43.refs_1_, bf16[1024,6656]{1,0:T(8,128)(2,1)} %refs_2_.35, bf16[1024,6656]{1,0:T(8,128)(2,1)} %refs_3_.17, ...), custom_call_target="tpu_custom_call", output_to_operand_aliasing={{}: (5, {})} | custom-call | flops 1000 | bytes 1000 | tf_op jit(solution)/shard_map/backward_products/pallas_call | solution.py:50
  191.2 6.2 %backward_products.21 = (f32[2,256,1024]{2,1,0:T(8,128)S(1)}, bf16[1024,6656]{1,0:T(8,128)(2,1)}, bf16[1024,6656]{1,0:T(8,128)(2,1)}, bf16[6656,1024]{1,0:T(8,128)(2,1)}) custom-call(bf16[3,128,768]{2,1,0:T(8,128)(2,1)S(1)} %choose.15.refs_6_.refs_0_, ...), custom_call_target="tpu_custom_call", output_to_operand_aliasing={{0}: (5, {}), {1}: (8, {}), {2}: (9, {}), {3}: (10, {})} | custom-call | flops 1000 | bytes 1000 | tf_op jit(solution)/shard_map/backward_products/pallas_call | solution.py:50
  197.5 6.2 %backward_products.22 = (f32[2,256,1024]{2,1,0:T(8,128)S(1)}, bf16[1024,6656]{1,0:T(8,128)(2,1)}, bf16[1024,6656]{1,0:T(8,128)(2,1)}, bf16[6656,1024]{1,0:T(8,128)(2,1)}) custom-call(bf16[3,128,768]{2,1,0:T(8,128)(2,1)S(1)} %choose.16.refs_11_.refs_0_, ...), custom_call_target="tpu_custom_call", output_to_operand_aliasing={{0}: (5, {}), {1}: (8, {}), {2}: (9, {}), {3}: (10, {})} | custom-call | flops 1000 | bytes 1000 | tf_op jit(solution)/shard_map/backward_products/pallas_call | solution.py:50
  219.5 4.0 %collective-permute-done.52 = bf16[2,64,1024]{2,1,0:T(8,128)(2,1)S(1)} collective-permute-done((bf16[2,64,1024]{2,1,0:T(8,128)(2,1)S(1)}, bf16[2,64,1024]{2,1,0:T(8,128)(2,1)S(1)}, u32[]{:S(2)}, u32[]{:S(2)}) %collective-permute-start.52) | collective-permute-done | bytes 262176 | tf_op jit(solution)/shard_map/ppermute | solution.py:381
  (185 shorter events, 110.5 us)
Async XLA Ops:
  5.2 15.7 %collective-permute-start.3 = (bf16[64,1024]{1,0:T(8,128)(2,1)}, bf16[64,1024]{1,0:T(8,128)(2,1)S(1)}, u32[]{:S(2)}, u32[]{:S(2)}) collective-permute-start(bf16[64,1024]{1,0:T(8,128)(2,1)} %refs_1_.16), channel_id=1, source_target_pairs={{0,1},{1,0},{2,3},{3,2},{4,5},{5,4},{6,7},{7,6},{8,9},{9,8},{10,11... | collective-permute-start | bytes 393224 | tf_op jit(solution)/shard_map/ppermute | solution.py:284
  29.0 18.5 %collective-permute-start.11 = (bf16[3,128,768]{2,1,0:T(8,128)(2,1)S(1)}, bf16[3,128,768]{2,1,0:T(8,128)(2,1)S(1)}, u32[]{:S(2)}, u32[]{:S(2)}) collective-permute-start(bf16[3,128,768]{2,1,0:T(8,128)(2,1)S(1)} %chip_sum.9.refs_2_.refs_0_), channel_id=1, source_target_pairs={{0,8},{4,12},{24,16},{28,20},{1,9},{5,13},{25,17},{29,21},{2,10},{... | collective-permute-start | bytes 1769480 | tf_op jit(solution)/shard_map/ppermute | solution.py:305
  44.9 19.0 %collective-permute-start.15 = (bf16[3,128,768]{2,1,0:T(8,128)(2,1)S(1)}, bf16[3,128,768]{2,1,0:T(8,128)(2,1)S(1)}, u32[]{:S(2)}, u32[]{:S(2)}) collective-permute-start(bf16[3,128,768]{2,1,0:T(8,128)(2,1)S(1)} %chip_sum.10.refs_5_.refs_0_), channel_id=1, source_target_pairs={{0,8},{4,12},{24,16},{28,20},{1,9},{5,13},{25,17},{29,21},{2,10},{... | collective-permute-start | bytes 1769480 | tf_op jit(solution)/shard_map/ppermute | solution.py:305
  59.1 23.0 %collective-permute-start.20 = (bf16[3,128,768]{2,1,0:T(8,128)(2,1)S(1)}, bf16[3,128,768]{2,1,0:T(8,128)(2,1)S(1)}, u32[]{:S(2)}, u32[]{:S(2)}) collective-permute-start(bf16[3,128,768]{2,1,0:T(8,128)(2,1)S(1)} %chip_sum.11.refs_2_.refs_0_), channel_id=1, source_target_pairs={{0,8},{4,12},{24,16},{28,20},{1,9},{5,13},{25,17},{29,21},{2,10},{... | collective-permute-start | bytes 1769480 | tf_op jit(solution)/shard_map/ppermute | solution.py:305
  64.1 19.7 %collective-permute-start.19 = (bf16[3,128,768]{2,1,0:T(8,128)(2,1)S(1)}, bf16[3,128,768]{2,1,0:T(8,128)(2,1)S(1)}, u32[]{:S(2)}, u32[]{:S(2)}) collective-permute-start(bf16[3,128,768]{2,1,0:T(8,128)(2,1)S(1)} %half_sum.10.refs_2_.refs_0_), channel_id=1, source_target_pairs={{8,16},{12,20},{16,8},{20,12},{9,17},{13,21},{17,9},{21,13},{10,18... | collective-permute-start | bytes 1769480 | tf_op jit(solution)/shard_map/ppermute | solution.py:313
  65.2 22.1 %collective-permute-start.18 = (bf16[3,128,768]{2,1,0:T(8,128)(2,1)S(1)}, bf16[3,128,768]{2,1,0:T(8,128)(2,1)}, u32[]{:S(2)}, u32[]{:S(2)}) collective-permute-start(bf16[3,128,768]{2,1,0:T(8,128)(2,1)S(1)} %activations.9.refs_2_.refs_0_), channel_id=1, source_target_pairs={{8,0},{12,4},{16,24},{20,28},{9,1},{13,5},{17,25},{21,29},{10,2},{... | collective-permute-start | bytes 1769480 | tf_op jit(solution)/shard_map/ppermute | solution.py:322
  72.5 17.3 %collective-permute-start.17 = (bf16[3,128,768]{2,1,0:T(8,128)(2,1)}, bf16[3,128,768]{2,1,0:T(8,128)(2,1)}, u32[]{:S(2)}, u32[]{:S(2)}) collective-permute-start(bf16[3,128,768]{2,1,0:T(8,128)(2,1)} %get-tuple-element.80), channel_id=1, source_target_pairs={{0,4},{4,0},{8,12},{12,8},{16,20},{20,16},{24,28},{28,24},{1,5},{5... | collective-permute-start | bytes 1769480 | tf_op jit(solution)/shard_map/ppermute | solution.py:299
  72.6 26.0 %collective-permute-start.26 = (bf16[3,128,768]{2,1,0:T(8,128)(2,1)}, bf16[3,128,768]{2,1,0:T(8,128)(2,1)}, u32[]{:S(2)}, u32[]{:S(2)}) collective-permute-start(bf16[3,128,768]{2,1,0:T(8,128)(2,1)} %chip_sum.12.refs_2_.refs_0_), channel_id=1, source_target_pairs={{0,8},{4,12},{24,16},{28,20},{1,9},{5,13},{25,17},{29,21},{2,10},{... | collective-permute-start | bytes 1769480 | tf_op jit(solution)/shard_map/ppermute | solution.py:305
  82.2 18.5 %collective-permute-start.25 = (bf16[3,128,768]{2,1,0:T(8,128)(2,1)S(1)}, bf16[3,128,768]{2,1,0:T(8,128)(2,1)}, u32[]{:S(2)}, u32[]{:S(2)}) collective-permute-start(bf16[3,128,768]{2,1,0:T(8,128)(2,1)S(1)} %half_sum.11.refs_2_.refs_0_), channel_id=1, source_target_pairs={{8,16},{12,20},{16,8},{20,12},{9,17},{13,21},{17,9},{21,13},{10,18... | collective-permute-start | bytes 1769480 | tf_op jit(solution)/shard_map/ppermute | solution.py:313
  87.3 17.5 %collective-permute-start.24 = (bf16[3,128,768]{2,1,0:T(8,128)(2,1)S(1)}, bf16[3,128,768]{2,1,0:T(8,128)(2,1)}, u32[]{:S(2)}, u32[]{:S(2)}) collective-permute-start(bf16[3,128,768]{2,1,0:T(8,128)(2,1)S(1)} %activations.10.refs_3_.refs_0_), channel_id=1, source_target_pairs={{8,0},{12,4},{16,24},{20,28},{9,1},{13,5},{17,25},{21,29},{10,2},{... | collective-permute-start | bytes 1769480 | tf_op jit(solution)/shard_map/ppermute | solution.py:322
  89.8 16.3 %collective-permute-start.23 = (bf16[3,128,768]{2,1,0:T(8,128)(2,1)S(1)}, bf16[3,128,768]{2,1,0:T(8,128)(2,1)S(1)}, u32[]{:S(2)}, u32[]{:S(2)}) collective-permute-start(bf16[3,128,768]{2,1,0:T(8,128)(2,1)S(1)} %choose.9.refs_2_.refs_0_), channel_id=1, source_target_pairs={{0,4},{4,0},{8,12},{12,8},{16,20},{20,16},{24,28},{28,24},{1,5},{5... | collective-permute-start | bytes 1769480 | tf_op jit(solution)/shard_map/ppermute | solution.py:333
  91.4 24.6 %collective-permute-start.22 = (bf16[3,128,768]{2,1,0:T(8,128)(2,1)}, bf16[3,128,768]{2,1,0:T(8,128)(2,1)S(1)}, u32[]{:S(2)}, u32[]{:S(2)}) collective-permute-start(bf16[3,128,768]{2,1,0:T(8,128)(2,1)} %chip_sum.13.refs_5_.refs_0_), channel_id=1, source_target_pairs={{0,8},{4,12},{24,16},{28,20},{1,9},{5,13},{25,17},{29,21},{2,10},{... | collective-permute-start | bytes 1769480 | tf_op jit(solution)/shard_map/ppermute | solution.py:305
  100.0 17.9 %collective-permute-start.31 = (bf16[3,128,768]{2,1,0:T(8,128)(2,1)S(1)}, bf16[3,128,768]{2,1,0:T(8,128)(2,1)S(1)}, u32[]{:S(2)}, u32[]{:S(2)}) collective-permute-start(bf16[3,128,768]{2,1,0:T(8,128)(2,1)S(1)} %half_sum.12.refs_2_.refs_0_), channel_id=1, source_target_pairs={{8,16},{12,20},{16,8},{20,12},{9,17},{13,21},{17,9},{21,13},{10,18... | collective-permute-start | bytes 1769480 | tf_op jit(solution)/shard_map/ppermute | solution.py:313
  102.1 17.4 %collective-permute-start.30 = (bf16[3,128,768]{2,1,0:T(8,128)(2,1)S(1)}, bf16[3,128,768]{2,1,0:T(8,128)(2,1)S(1)}, u32[]{:S(2)}, u32[]{:S(2)}) collective-permute-start(bf16[3,128,768]{2,1,0:T(8,128)(2,1)S(1)} %activations.11.refs_3_.refs_0_), channel_id=1, source_target_pairs={{8,0},{12,4},{16,24},{20,28},{9,1},{13,5},{17,25},{21,29},{10,2},{... | collective-permute-start | bytes 1769480 | tf_op jit(solution)/shard_map/ppermute | solution.py:322
  106.1 24.4 %collective-permute-start.28 = (bf16[3,128,768]{2,1,0:T(8,128)(2,1)}, bf16[3,128,768]{2,1,0:T(8,128)(2,1)S(1)}, u32[]{:S(2)}, u32[]{:S(2)}) collective-permute-start(bf16[3,128,768]{2,1,0:T(8,128)(2,1)} %chip_sum.14.refs_2_.refs_0_), channel_id=1, source_target_pairs={{0,8},{4,12},{24,16},{28,20},{1,9},{5,13},{25,17},{29,21},{2,10},{... | collective-permute-start | bytes 1769480 | tf_op jit(solution)/shard_map/ppermute | solution.py:305
  118.2 17.2 %collective-permute-start.36 = (bf16[3,128,768]{2,1,0:T(8,128)(2,1)S(1)}, bf16[3,128,768]{2,1,0:T(8,128)(2,1)S(1)}, u32[]{:S(2)}, u32[]{:S(2)}) collective-permute-start(bf16[3,128,768]{2,1,0:T(8,128)(2,1)S(1)} %activations.12.refs_3_.refs_0_), channel_id=1, source_target_pairs={{8,0},{12,4},{16,24},{20,28},{9,1},{13,5},{17,25},{21,29},{10,2},{... | collective-permute-start | bytes 1769480 | tf_op jit(solution)/shard_map/ppermute | solution.py:322
  119.6 15.9 %collective-permute-start.35 = (bf16[3,128,768]{2,1,0:T(8,128)(2,1)S(1)}, bf16[3,128,768]{2,1,0:T(8,128)(2,1)S(1)}, u32[]{:S(2)}, u32[]{:S(2)}) collective-permute-start(bf16[3,128,768]{2,1,0:T(8,128)(2,1)S(1)} %choose.11.refs_11_.refs_0_), channel_id=1, source_target_pairs={{0,4},{4,0},{8,12},{12,8},{16,20},{20,16},{24,28},{28,24},{1,5},{5... | collective-permute-start | bytes 1769480 | tf_op jit(solution)/shard_map/ppermute | solution.py:333
  119.7 25.4 %collective-permute-start.34 = (bf16[3,128,768]{2,1,0:T(8,128)(2,1)S(1)}, bf16[3,128,768]{2,1,0:T(8,128)(2,1)S(1)}, u32[]{:S(2)}, u32[]{:S(2)}) collective-permute-start(bf16[3,128,768]{2,1,0:T(8,128)(2,1)S(1)} %copy-done.7), channel_id=1, source_target_pairs={{0,8},{4,12},{24,16},{28,20},{1,9},{5,13},{25,17},{29,21},{2,10},{... | collective-permute-start | bytes 1769480 | tf_op jit(solution)/shard_map/ppermute | solution.py:305
  132.7 17.3 %collective-permute-start.32 = (bf16[3,128,768]{2,1,0:T(8,128)(2,1)S(1)}, bf16[3,128,768]{2,1,0:T(8,128)(2,1)S(1)}, u32[]{:S(2)}, u32[]{:S(2)}) collective-permute-start(bf16[3,128,768]{2,1,0:T(8,128)(2,1)S(1)} %activations.13.refs_3_.refs_0_), channel_id=1, source_target_pairs={{8,0},{12,4},{16,24},{20,28},{9,1},{13,5},{17,25},{21,29},{10,2},{... | collective-permute-start | bytes 1769480 | tf_op jit(solution)/shard_map/ppermute | solution.py:322
  135.5 18.7 %collective-permute-start.41 = (bf16[3,128,768]{2,1,0:T(8,128)(2,1)S(1)}, bf16[3,128,768]{2,1,0:T(8,128)(2,1)S(1)}, u32[]{:S(2)}, u32[]{:S(2)}) collective-permute-start(bf16[3,128,768]{2,1,0:T(8,128)(2,1)S(1)} %chip_sum.16.refs_2_.refs_0_), channel_id=1, source_target_pairs={{0,8},{4,12},{24,16},{28,20},{1,9},{5,13},{25,17},{29,21},{2,10},{... | collective-permute-start | bytes 1769480 | tf_op jit(solution)/shard_map/ppermute | solution.py:305
  146.2 17.3 %collective-permute-start.39 = (bf16[3,128,768]{2,1,0:T(8,128)(2,1)S(1)}, bf16[3,128,768]{2,1,0:T(8,128)(2,1)S(1)}, u32[]{:S(2)}, u32[]{:S(2)}) collective-permute-start(bf16[3,128,768]{2,1,0:T(8,128)(2,1)S(1)} %activations.14.refs_3_.refs_0_), channel_id=1, source_target_pairs={{8,0},{12,4},{16,24},{20,28},{9,1},{13,5},{17,25},{21,29},{10,2},{... | collective-permute-start | bytes 1769480 | tf_op jit(solution)/shard_map/ppermute | solution.py:322
  159.5 17.4 %collective-permute-start.44 = (bf16[3,128,768]{2,1,0:T(8,128)(2,1)S(1)}, bf16[3,128,768]{2,1,0:T(8,128)(2,1)S(1)}, u32[]{:S(2)}, u32[]{:S(2)}) collective-permute-start(bf16[3,128,768]{2,1,0:T(8,128)(2,1)S(1)} %activations.15.refs_3_.refs_0_), channel_id=1, source_target_pairs={{8,0},{12,4},{16,24},{20,28},{9,1},{13,5},{17,25},{21,29},{10,2},{... | collective-permute-start | bytes 1769480 | tf_op jit(solution)/shard_map/ppermute | solution.py:322
  168.3 21.3 %collective-permute-start.47 = (bf16[3,128,768]{2,1,0:T(8,128)(2,1)S(1)}, bf16[3,128,768]{2,1,0:T(8,128)(2,1)S(1)}, u32[]{:S(2)}, u32[]{:S(2)}) collective-permute-start(bf16[3,128,768]{2,1,0:T(8,128)(2,1)S(1)} %activations.16.refs_3_.refs_0_), channel_id=1, source_target_pairs={{8,0},{12,4},{16,24},{20,28},{9,1},{13,5},{17,25},{21,29},{10,2},{... | collective-permute-start | bytes 1769480 | tf_op jit(solution)/shard_map/ppermute | solution.py:322
  169.6 18.2 %collective-permute-start.42 = (bf16[3,128,512]{2,1,0:T(8,128)(2,1)S(1)}, bf16[3,128,512]{2,1,0:T(8,128)(2,1)S(1)}, u32[]{:S(2)}, u32[]{:S(2)}) collective-permute-start(bf16[3,128,512]{2,1,0:T(8,128)(2,1)S(1)} %half_sum.17.refs_2_.refs_0_), channel_id=1, source_target_pairs={{8,16},{12,20},{16,8},{20,12},{9,17},{13,21},{17,9},{21,13},{10,18... | collective-permute-start | bytes 1179656 | tf_op jit(solution)/shard_map/ppermute | solution.py:313
  (46 other events, 424.0 us)
